TPU v7x, 256 devices: a whole 4x4x8 slice. The times are simulated.
256 devices in a mesh: dp: 128 (over z, x_hi, y, core), mp: 2 (over x_lo).
Axes of the slice: x: 4 (x_hi: 2, x_lo: 2; x = x_hi * 2 + x_lo), y: 4, z: 8, core: 2. Of those that a mesh axis runs over, the one named last changes fastest.
Arguments:
- image_tokens: bfloat16 [2048, 64, 1536], P('dp'), may hold values from -24 to 24
- text_tokens: bfloat16 [2048, 32, 1536], P('dp'), may hold values from -24 to 24
- image_weight: bfloat16 [1536, 1536], P(None, 'mp'), may hold values from -0.15625 to 0.15625
- text_weight: bfloat16 [1536, 1536], P(None, 'mp'), may hold values from -0.15625 to 0.15625
- logit_scale: float32 [1], replicated, may hold values from 6 to 14
- logit_bias: float32 [1], replicated, may hold values from -8 to -5
- loss_scale: float32 [1], replicated, may hold values from 256 to 4096
- valid_count: int32 [128], P('dp'), may hold values from 3 to 16, as said below
Outputs:
- loss: float32 [], replicated
- image_weight_grad: float32 [1536, 1536], P('dp', 'mp')
- text_weight_grad: float32 [1536, 1536], P('dp', 'mp')
Inputs may be any that keep to these rules, and one draw needn't show every extreme that they name: `valid_count`: at least one index of dp has all 16 pairs valid.
All inputs are finite; a program needn't handle non-finite values.
Results may differ from a plain program's by a relative error of at most 0.0014.
Values may be sent and summed in bfloat16 or wider, within the bound.
A program may use at most 128 MiB of HBM per device.

v0:
```python
import jax
import jax.numpy as jnp
from jax import lax
from jax.sharding import PartitionSpec as P


def gelu_slope(values):
    return jax.jvp(
        lambda inner: jax.nn.gelu(inner, approximate=True), (values,), (jnp.ones_like(values),)
    )[1]


def tower_block(tokens, weight, offset):
    flat_tokens = tokens.reshape(-1, tokens.shape[2])
    preact = jnp.dot(flat_tokens, weight, preferred_element_type=jnp.float32)
    residual = lax.dynamic_slice_in_dim(flat_tokens, offset, weight.shape[1], 1).astype(jnp.float32)
    hidden = residual + jax.nn.gelu(preact, approximate=True)
    pooled = jnp.mean(hidden.reshape(tokens.shape[0], tokens.shape[1], -1), axis=1)
    return (flat_tokens, preact, pooled)


def contract_rows(left_rows, right_rows):
    return lax.dot_general(
        left_rows, right_rows, (((0,), (0,)), ((), ())), preferred_element_type=jnp.float32
    )


def row_products(left_rows, right_rows):
    return lax.dot_general(
        left_rows, right_rows, (((1,), (1,)), ((), ())), preferred_element_type=jnp.float32
    )


def weight_terms(flat_tokens, grad_preact):
    return contract_rows(flat_tokens, grad_preact)


def text_terms_of(dlogit, image_bf):
    return contract_rows(dlogit, image_bf)


def body(
    image_tokens,
    text_tokens,
    image_weight,
    text_weight,
    logit_scale,
    logit_bias,
    loss_scale,
    valid_count,
):
    samples_here = image_tokens.shape[0]
    half_width = image_weight.shape[1]
    cycle_size = lax.axis_size("dp")
    cycle_place = lax.axis_index("dp")
    model_place = lax.axis_index("mp")
    half_start = model_place * half_width
    image_flat, image_preact, image_pooled = tower_block(image_tokens, image_weight, half_start)
    text_flat, text_preact, text_pooled = tower_block(text_tokens, text_weight, half_start)
    image_sq, text_sq = lax.psum(
        (jnp.sum(image_pooled * image_pooled, axis=1), jnp.sum(text_pooled * text_pooled, axis=1)),
        "mp",
    )
    image_norm = jnp.sqrt(image_sq + 1e-06)
    text_norm = jnp.sqrt(text_sq + 1e-06)
    image_unit = image_pooled / image_norm[:, None]
    text_unit = text_pooled / text_norm[:, None]
    image_bf = image_unit.astype(jnp.bfloat16)
    text_bf = text_unit.astype(jnp.bfloat16)
    all_counts = lax.all_gather(valid_count, "dp", axis=0, tiled=True)
    total_count = jnp.sum(all_counts).astype(jnp.float32)
    logit_mult = logit_scale[0]
    offset_term = logit_bias[0]
    grad_coeff = loss_scale[0] / total_count
    positions = jnp.arange(samples_here, dtype=jnp.int32)
    own_usable = positions < lax.dynamic_index_in_dim(all_counts, cycle_place, 0, False)
    own_rows = cycle_place * samples_here + positions
    all_columns = samples_here * cycle_size
    image_full, text_full = (
        lax.all_gather(image_bf, "mp", axis=1, tiled=True),
        lax.all_gather(text_bf, "mp", axis=1, tiled=True),
    )
    all_text = lax.all_gather(text_full, "dp", axis=0, tiled=True)
    columns = jnp.arange(all_columns, dtype=jnp.int32)
    logits = logit_mult * row_products(image_full, all_text) + offset_term
    col_usable = columns % samples_here < jnp.take(all_counts, columns // samples_here)
    pair_sign = jnp.where(columns[None, :] == own_rows[:, None], 1.0, -1.0).astype(jnp.float32)
    weighting = own_usable[:, None] & col_usable[None, :]
    margin = -pair_sign * logits
    loss_part = jnp.sum(jnp.where(weighting, jax.nn.softplus(margin), 0.0))
    dlogit = (jnp.where(weighting, -pair_sign * jax.nn.sigmoid(margin), 0.0) * grad_coeff).astype(
        jnp.bfloat16
    )
    loss_local, dlogit = (loss_part, dlogit)
    own_text = lax.dynamic_slice_in_dim(all_text, half_start, half_width, 1)
    image_raw = jnp.dot(dlogit, own_text, preferred_element_type=jnp.float32)
    text_raw = lax.psum_scatter(
        text_terms_of(dlogit, image_bf), "dp", scatter_dimension=0, tiled=True
    )
    loss = lax.psum(loss_local / total_count, "dp")
    image_grad = logit_mult * image_raw
    text_grad = logit_mult * text_raw
    image_rad, text_rad = lax.psum(
        (jnp.sum(image_unit * image_grad, axis=1), jnp.sum(text_unit * text_grad, axis=1)), "mp"
    )
    image_gp = (image_grad - image_unit * image_rad[:, None]) / image_norm[:, None]
    text_gp = (text_grad - text_unit * text_rad[:, None]) / text_norm[:, None]
    image_count = image_tokens.shape[1]
    text_count = text_tokens.shape[1]
    image_slope = gelu_slope(image_preact.reshape(samples_here, image_count, half_width))
    text_slope = gelu_slope(text_preact.reshape(samples_here, text_count, half_width))
    image_gpre = (
        (image_gp[:, None, :] / image_count * image_slope)
        .astype(jnp.bfloat16)
        .reshape(-1, half_width)
    )
    text_gpre = (
        (text_gp[:, None, :] / text_count * text_slope).astype(jnp.bfloat16).reshape(-1, half_width)
    )
    image_weight_grad = lax.psum_scatter(
        weight_terms(image_flat, image_gpre), "dp", scatter_dimension=0, tiled=True
    )
    text_weight_grad = lax.psum_scatter(
        weight_terms(text_flat, text_gpre), "dp", scatter_dimension=0, tiled=True
    )
    return (loss, image_weight_grad, text_weight_grad)


def solution(mesh):
    placed = (
        P("dp", None, None),
        P("dp", None, None),
        P(None, "mp"),
        P(None, "mp"),
        P(),
        P(),
        P(),
        P("dp"),
    )
    return jax.shard_map(
        body,
        mesh=mesh,
        in_specs=placed,
        out_specs=(P(), P("dp", "mp"), P("dp", "mp")),
        check_vma=False,
    )
```

profile of v0, /device:TPU:1, one launch (start us, length us, event | category | flops | bytes accessed | tf_op | source)
XLA Modules:
  0.0 1760.2 jit_solution(17081759434492923223)
XLA Ops:
  7.2 5.3 bitcast_reduce_fusion.1
  12.6 4.9 bitcast_reduce_fusion
  17.6 4.4 all-reduce.5
  22.0 3.5 all_gather.14
  28.7 0.8 dynamic-update-slice
  29.5 26.7 %all-reduce = s32[128]{0:T(128)S(1)} all-reduce(s32[128]{0:T(128)S(1)} %dynamic-update-slice), channel_id=1, replica_groups=mesh['dp'=128,'mp'=2] {'dp'}, use_global_device_ids=true, to_apply=%add | all-reduce | flops 128 | bytes 1024
  56.3 0.7 reduce_sum.77
  58.3 12.6 gather_fusion
  71.0 3.3 all_gather.13
  75.1 80.8 %all-gather.2.cloned.1.call-done = bf16[2048,1536]{1,0:T(8,128)(2,1)} async-done(((bf16[16,1536]{1,0:T(8,128)(2,1)}), bf16[2048,1536]{1,0:T(8,128)(2,1)}) %all-gather.2.cloned.1.call-update) | async-done | bytes 6291472 | tf_op jit(solution)/shard_map/all_gather | solution.py:83
  155.9 5.2 fusion.61
  161.1 3.7 fusion.86
  164.9 2.6 multiply_reduce_fusion.1
  167.5 262.9 %reduce-scatter.4.cloned.1.call-done = f32[16,768]{1,0:T(8,128)} async-done(((f32[2048,768]{1,0:T(8,128)}), f32[16,768]{1,0:T(8,128)}) %reduce-scatter.4.cloned.1.call-update) | async-done | bytes 49168 | tf_op jit(solution)/shard_map/reduce_scatter | solution.py:97
  430.4 1.0 multiply_reduce_fusion
  431.4 4.0 all-reduce.4
  435.5 9.1 convolution_bitcast_fusion.1
  444.7 4.2 convolution_bitcast_fusion
  450.2 330.2 %psum.37 = f32[]{:T(128)} all-reduce(f32[]{:T(128)S(6)} %div.81), channel_id=1, replica_groups=mesh['dp'=128,'mp'=2] {'dp'}, use_global_device_ids=true, to_apply=%region_8.9 | all-reduce | flops 1 | bytes 8 | tf_op jit(solution)/shard_map/psum | solution.py:100
  780.4 969.1 %all-reduce.8.cloned.1.call-done = (f32[1536,768]{0,1:T(8,128)}, f32[1536,768]{0,1:T(8,128)}) async-done(((f32[1536,768]{0,1:T(8,128)}, f32[1536,768]{0,1:T(8,128)}), (f32[1536,768]{0,1:T(8,128)}, f32[1536,768]{0,1:T(8,128)})) %all-reduce.8.cloned.1.call-update) | async-done | bytes 9437200
  1749.5 1.3 constant_dynamic-slice_fusion.1
  1750.8 1.3 constant_dynamic-slice_fusion
  1752.1 0.8 copy.16
  1752.9 0.8 copy.15
  (33 shorter events, 2.5 us)
Async XLA Ops:
  7.2 5.4 copy-start
  7.2 148.7 %all-gather.2.cloned.1.call-start = ((), (), s32[]{:S(2)}) async-start(), calls=%async_computation.1 | async-start | bytes 6340608 | tf_op jit(solution)/shard_map/all_gather | solution.py:83
  7.2 5.3 copy-start.3
  12.6 15.6 copy-start.2
  25.5 404.9 %reduce-scatter.4.cloned.1.call-start = ((), (), s32[]{:S(2)}) async-start(), calls=%async_computation.2 | async-start | bytes 6340608 | tf_op jit(solution)/shard_map/reduce_scatter | solution.py:97
  164.8 1584.6 %all-reduce.8.cloned.1.call-start = ((), (), s32[]{:S(2)}) async-start(), calls=%async_computation.3 | async-start | bytes 18874368
  435.4 9.1 copy-start.1
  435.4 9.2 copy-start.4
  435.4 9.2 copy-start.5
Sparse Core Ops, SparseCore 0:
  25.6 130.2 all-gather.1
  165.0 265.3 reduce-scatter.3
  449.1 1300.3 all-reduce.7
where the time goes:
time: 1770 us; the launch traced here: 1760 us
  waiting for transfers between devices  1310 us (74%)
  blocking collectives  372 us (21%)
  matrix products  35 us (2%)
  local copies, waits for them, and re-layouts  18.7 us (1%)
  between operations  18.5 us (1%)
    unnamed x4, waiting for transfers between devices  969 us
    psum x1, blocking collectives, body(): loss = lax.psum(loss_local / total_count, 'dp')  330 us
    reduce_scatter x1, waiting for transfers between devices, body(): lax.psum_scatter(text_terms_of(dlogit, image_bf), 'dp', scatter_dimension...  263 us
    all_gather x1, waiting for transfers between devices, body(): all_text = lax.all_gather(text_full, 'dp', axis=0, tiled=True)  80.8 us
  transfers between devices with their start and end apart: 3, of which 3 were waited for; matrix products, arithmetic and copies ran while one was open for 1% of the time, Pallas kernels for 0%

commit v1 on v0

v1 whole, which is shorter than its diff:
```python
import jax
import jax.numpy as jnp
from jax import lax
from jax.experimental import pallas as pl
from jax.experimental.pallas import tpu as pltpu
from jax.sharding import PartitionSpec as P

MESH = pl.DeviceIdType.MESH
F32 = jnp.float32
BF16 = jnp.bfloat16
NZ, NY, NX, NC = 8, 4, 4, 2
D = 1536
H = 768
EXT = 128
ZROWS = D // NZ
OWN = 24


def place():
    dp = lax.axis_index("dp")
    lo = lax.axis_index("mp")
    c = lax.rem(dp, 2)
    y = lax.rem(lax.div(dp, 2), 4)
    xh = lax.rem(lax.div(dp, 8), 2)
    z = lax.div(dp, 16)
    return z, y, xh * 2 + lo, c


def device_at(z, y, x, c):
    return (((z * 2 + lax.div(x, 2)) * 4 + y) * 2 + c, lax.rem(x, 2))


def slot_of(x, c):
    return (lax.div(x, 2) * 2 + c) * 2 + lax.rem(x, 2)


def send_to(src, dst, send_sem, recv_sem, device):
    return pltpu.make_async_remote_copy(
        src_ref=src,
        dst_ref=dst,
        send_sem=send_sem,
        recv_sem=recv_sem,
        device_id=device,
        device_id_type=MESH,
    )


def greet(devices):
    barrier = pltpu.get_barrier_semaphore()
    for device in devices:
        pl.semaphore_signal(barrier, inc=1, device_id=device, device_id_type=MESH)
    pl.semaphore_wait(barrier, len(devices))


GROUP = [(dx, dc) for dx in range(NX) for dc in range(NC) if (dx, dc) != (0, 0)]


def dot_t(a, b):
    return lax.dot_general(a, b, (((1,), (1,)), ((), ())), preferred_element_type=F32)


def pair_kernel(
    pooled_ref,
    count_ref,
    scale_ref,
    bias_ref,
    loss_scale_ref,
    grad_ref,
    loss_ref,
    other,
    counts,
    plane,
    group,
    parts,
    landed,
    unit_own,
    s_other,
    r_other,
    s_count,
    r_count,
    s_group,
    r_group,
    s_y,
    r_y,
    s_up,
    r_up,
    s_down,
    r_down,
    s_part,
    r_part,
):
    z, y, x, c = place()
    lo = lax.rem(x, 2)
    me = slot_of(x, c)
    zu, zd = lax.rem(z + 1, NZ), lax.rem(z + NZ - 1, NZ)
    up, down = device_at(zu, y, x, c), device_at(zd, y, x, c)
    members = {(dx, dc): device_at(z, y, lax.rem(x + dx, NX), lax.rem(c + dc, NC)) for dx, dc in GROUP}
    sources = {(dx, dc): (lax.rem(x + NX - dx, NX), lax.rem(c + dc, NC)) for dx, dc in GROUP}
    y_peers = [device_at(z, lax.rem(y + j, NY), x, c) for j in range(1, NY)]
    partner = device_at(z, y, lax.div(x, 2) * 2 + 1 - lo, c)
    greet([members[key] for key in GROUP] + y_peers + [up, down])

    half_copy = send_to(pooled_ref, other, s_other, r_other, partner)
    half_copy.start()
    counts[me] = count_ref[...]
    count_copies = []
    for n, key in enumerate(GROUP):
        copy = send_to(counts.at[me], counts.at[me], s_count.at[n], r_count.at[n], members[key])
        copy.start()
        count_copies.append(copy)
    mine = pooled_ref[...]
    own_sq = jnp.sum(mine * mine, axis=1, keepdims=True)
    half_copy.wait_recv()
    theirs = other[...]
    norm = jnp.sqrt(own_sq + jnp.sum(theirs * theirs, axis=1, keepdims=True) + 1e-6)
    unit_mine = mine / norm
    unit_theirs = theirs / norm
    unit_own[...] = unit_mine
    first = lo == 0
    low = jnp.where(first, unit_mine, unit_theirs)
    high = jnp.where(first, unit_theirs, unit_mine)
    for n, key in enumerate(GROUP):
        sx, sc = sources[key]
        slot = slot_of(sx, sc)
        send_to(counts.at[slot], counts.at[slot], s_count.at[n], r_count.at[n], members[key]).wait_recv()
    row_total = jnp.sum(counts[...], axis=0)[0:1, :] * 0.5
    own_count = count_ref[0:1, :]
    own_low = jnp.where(first, low[0:16], low[16:32])
    own_high = jnp.where(first, high[0:16], high[16:32])
    sample = lax.rem(lax.broadcasted_iota(jnp.int32, (16, EXT), 0), 8) + 8 * lo
    lane = lax.broadcasted_iota(jnp.int32, (16, EXT), 1)
    usable = jnp.where(sample.astype(F32) < own_count, 1.0, 0.0)
    extra = jnp.where(lane < EXT // 2, usable, jnp.broadcast_to(row_total, (16, EXT)))
    block = jnp.concatenate([own_low.astype(BF16), own_high.astype(BF16), extra.astype(BF16)], axis=1)
    plane[z, y] = block
    group[me] = block

    y_copies = []
    for j in range(1, NY):
        copy = send_to(plane.at[z, y], plane.at[z, y], s_y.at[j - 1], r_y.at[j - 1], y_peers[j - 1])
        copy.start()
        y_copies.append(copy)
    z_copies = []

    def pass_up(step, j, zs, ys):
        copy = send_to(plane.at[zs, ys], plane.at[zs, ys], s_up.at[step, j], r_up.at[step, j], up)
        copy.start()
        z_copies.append(copy)

    def pass_down(step, j, zs, ys):
        copy = send_to(plane.at[zs, ys], plane.at[zs, ys], s_down.at[step, j], r_down.at[step, j], down)
        copy.start()
        z_copies.append(copy)

    pass_up(0, 0, z, y)
    pass_down(0, 0, z, y)
    group_copies = []
    for n, key in enumerate(GROUP):
        copy = send_to(group.at[me], group.at[me], s_group.at[n], r_group.at[n], members[key])
        copy.start()
        group_copies.append(copy)
    for j in range(1, NY):
        ys = lax.rem(y + NY - j, NY)
        send_to(plane.at[z, ys], plane.at[z, ys], s_y.at[j - 1], r_y.at[j - 1], up).wait_recv()
        pass_up(0, j, z, ys)
        pass_down(0, j, z, ys)
    for step in range(4):
        for j in range(NY):
            ys = lax.rem(y + NY - j, NY)
            if step < 3 or j < 2:
                zs = lax.rem(z + NZ - step - 1, NZ)
                send_to(plane.at[zs, ys], plane.at[zs, ys], s_up.at[step, j], r_up.at[step, j], up).wait_recv()
                if step < 2 or (step == 2 and j < 2):
                    pass_up(step + 1, j, zs, ys)
            if step < 3 or j >= 2:
                zs = lax.rem(z + step + 1, NZ)
                send_to(plane.at[zs, ys], plane.at[zs, ys], s_down.at[step, j], r_down.at[step, j], down).wait_recv()
                if step < 2 or (step == 2 and j >= 2):
                    pass_down(step + 1, j, zs, ys)
    for n, key in enumerate(GROUP):
        sx, sc = sources[key]
        slot = slot_of(sx, sc)
        send_to(group.at[slot], group.at[slot], s_group.at[n], r_group.at[n], members[key]).wait_recv()

    rows = group[...].reshape(8 * 16, D + EXT)
    cols = plane[...].reshape(32 * 16, D + EXT)
    row_main, col_main = rows[:, :D], cols[:, :D]
    logit_mult = scale_ref[0]
    logits = logit_mult * dot_t(row_main, col_main) + bias_ref[0]
    pick = lax.broadcasted_iota(jnp.int32, (16, EXT), 0) * (EXT // 2)
    pick = jnp.where(pick == lax.broadcasted_iota(jnp.int32, (16, EXT), 1), 1.0, 0.0).astype(BF16)
    col_extra = dot_t(pick, cols[:, D:])
    total = jnp.sum(col_extra[1:2, :]) * (1.0 / 16.0)
    col_usable = col_extra[0:1, :]
    row_usable = rows[:, D : D + 1].astype(F32)
    shape = (8 * 16, 32 * 16)
    r = lax.broadcasted_iota(jnp.int32, shape, 0)
    q = lax.broadcasted_iota(jnp.int32, shape, 1)
    r_text = lax.rem(lax.div(r, 8), 2)
    q_text = lax.rem(lax.div(q, 8), 2)
    same = (lax.div(r, 16) == me) & (lax.div(q, 16) == z * NY + y) & (lax.rem(r, 8) == lax.rem(q, 8))
    used = (row_usable * col_usable > 0.5) & (r_text != q_text)
    sign = jnp.where(same, 1.0, -1.0)
    margin = -sign * logits
    soft = jnp.maximum(margin, 0.0) + jnp.log1p(jnp.exp(-jnp.abs(margin)))
    loss = jnp.sum(jnp.where(used & (r_text == 0), soft, 0.0), axis=1, keepdims=True)
    loss_ref[...] = jnp.broadcast_to(jnp.sum(loss, axis=0, keepdims=True) / total, (8, 128))
    coeff = loss_scale_ref[0] / total
    dlogit = (jnp.where(used, -sign * jax.nn.sigmoid(margin), 0.0) * coeff).astype(BF16)
    grad = logit_mult * jnp.dot(dlogit, col_main, preferred_element_type=F32)
    radial = jnp.sum(row_main.astype(F32) * grad, axis=1, keepdims=True)
    radial = jnp.broadcast_to(radial, (8 * 16, EXT))
    for pair in range(4):
        for half in range(2):
            band = slice(pair * 32, pair * 32 + 32)
            parts[pair, half, :, :H] = grad[band, half * H : half * H + H]
            parts[pair, half, :, H:] = radial[band]

    part_copies = []
    for n, key in enumerate(GROUP):
        dx, dc = key
        tx, tc = lax.rem(x + dx, NX), lax.rem(c + dc, NC)
        copy = send_to(
            parts.at[lax.div(tx, 2) * 2 + tc, lax.rem(tx, 2)],
            landed.at[me],
            s_part.at[n],
            r_part.at[n],
            members[key],
        )
        copy.start()
        part_copies.append(copy)
    total_grad = parts[lax.div(x, 2) * 2 + c, lo]
    for n, key in enumerate(GROUP):
        sx, sc = sources[key]
        slot = slot_of(sx, sc)
        send_to(landed.at[slot], landed.at[slot], s_part.at[n], r_part.at[n], members[key]).wait_recv()
        total_grad = total_grad + landed[slot]
    grad_ref[...] = (total_grad[:, :H] - unit_own[...] * total_grad[:, H : H + 1]) / norm
    for copy in [half_copy] + count_copies + y_copies + z_copies + group_copies + part_copies:
        copy.wait_send()


def pair_gradients(pooled, count, logit_scale, logit_bias, loss_scale):
    dma = pltpu.SemaphoreType.DMA
    vmem = pl.BlockSpec(memory_space=pltpu.VMEM)
    smem = pl.BlockSpec(memory_space=pltpu.SMEM)
    return pl.pallas_call(
        pair_kernel,
        out_shape=(jax.ShapeDtypeStruct((32, H), F32), jax.ShapeDtypeStruct((8, 128), F32)),
        in_specs=[vmem, vmem, smem, smem, smem],
        out_specs=(vmem, vmem),
        scratch_shapes=[
            pltpu.VMEM((32, H), F32),
            pltpu.VMEM((8, 8, 128), F32),
            pltpu.VMEM((NZ, NY, 16, D + EXT), BF16),
            pltpu.VMEM((8, 16, D + EXT), BF16),
            pltpu.VMEM((4, 2, 32, H + EXT), F32),
            pltpu.VMEM((8, 32, H + EXT), F32),
            pltpu.VMEM((32, H), F32),
            dma, dma,
            dma((7,)), dma((7,)),
            dma((7,)), dma((7,)),
            dma((3,)), dma((3,)),
            dma((4, 4)), dma((4, 4)),
            dma((4, 4)), dma((4, 4)),
            dma((7,)), dma((7,)),
        ],
        compiler_params=pltpu.CompilerParams(
            collective_id=1, has_side_effects=True, vmem_limit_bytes=48 * 1024 * 1024
        ),
    )(pooled, count, logit_scale, logit_bias, loss_scale)


YX = [(dxh, j) for dxh in range(2) for j in range(NY) if (dxh, j) != (0, 0)]


def reduce_kernel(
    image_ref,
    text_ref,
    loss_ref,
    out_ref,
    loss_out_ref,
    terms,
    sibling,
    up_out,
    up_in,
    down_out,
    down_in,
    owned,
    near_in,
    final,
    loss_group,
    loss_y,
    loss_z,
    loss_stage,
    s_load,
    s_sib,
    r_sib,
    s_up,
    r_up,
    s_down,
    r_down,
    s_near,
    r_near,
    s_final,
    r_final,
    s_lg,
    r_lg,
    s_ly,
    r_ly,
    s_lz,
    r_lz,
):
    z, y, x, c = place()
    xh, lo = lax.div(x, 2), lax.rem(x, 2)
    up = device_at(lax.rem(z + 1, NZ), y, x, c)
    down = device_at(lax.rem(z + NZ - 1, NZ), y, x, c)
    twin = device_at(z, y, x, 1 - c)
    members = {(dx, dc): device_at(z, y, lax.rem(x + dx, NX), lax.rem(c + dc, NC)) for dx, dc in GROUP}
    near = {
        (dxh, j): device_at(z, lax.rem(y + j, NY), lax.rem(xh + dxh, 2) * 2 + lo, c) for dxh, j in YX
    }
    z_peers = [device_at(lax.rem(z + k, NZ), y, x, c) for k in range(1, NZ)]

    order = [4, 3, 5, 2, 6, 1, 7, 0]
    loads = []
    for n, k in enumerate(order):
        t = lax.rem(z + k, NZ)
        pair = [
            pltpu.make_async_copy(ref.at[t], terms.at[i, t], s_load.at[i, n])
            for i, ref in enumerate((image_ref, text_ref))
        ]
        for load in pair:
            load.start()
        loads.append(pair)
    loss_group[0] = loss_ref[...]
    greet(
        [members[key] for key in GROUP]
        + [near[key] for key in YX if key != (1, 0)]
        + z_peers
    )
    copies = []

    def start(copy):
        copy.start()
        copies.append(copy)

    for n, key in enumerate(GROUP):
        start(send_to(loss_group.at[0], loss_group.at[n + 1], s_lg.at[n], r_lg.at[n], members[key]))
    for n, k in enumerate(order):
        t = lax.rem(z + k, NZ)
        for load in loads[n]:
            load.wait()
        start(send_to(terms.at[1 - c, t], sibling.at[t], s_sib.at[n], r_sib.at[n], twin))

    def chunk(n):
        t = lax.rem(z + order[n], NZ)
        send_to(sibling.at[t], sibling.at[t], s_sib.at[n], r_sib.at[n], twin).wait_recv()
        return t

    half = H // 2
    t = chunk(0)
    up_out[0, :, :half] = terms[c, t, :, :half] + sibling[t, :, :half]
    start(send_to(up_out.at[0, :, pl.ds(0, half)], up_in.at[0, :, pl.ds(0, half)], s_up.at[0], r_up.at[0], up))
    down_out[0, :, half:] = terms[c, t, :, half:] + sibling[t, :, half:]
    start(send_to(down_out.at[0, :, pl.ds(half, half)], down_in.at[0, :, pl.ds(half, half)], s_down.at[0], r_down.at[0], down))
    for n, key in enumerate(GROUP):
        send_to(loss_group.at[0], loss_group.at[n + 1], s_lg.at[n], r_lg.at[n], members[key]).wait_recv()
    loss_y[0] = jnp.sum(loss_group[...], axis=0)
    for j in range(1, NY):
        start(send_to(loss_y.at[0], loss_y.at[j], s_ly.at[j - 1], r_ly.at[j - 1], near[(0, j)]))
    for step in range(1, 4):
        t = chunk(2 * step - 1)
        up_out[step] = terms[c, t] + sibling[t]
        if step == 1:
            send_to(up_out.at[0, :, pl.ds(0, half)], up_in.at[0, :, pl.ds(0, half)], s_up.at[0], r_up.at[0], up).wait_recv()
            up_out[step, :, :half] += up_in[0, :, :half]
        else:
            send_to(up_out.at[step - 1], up_in.at[step - 1], s_up.at[step - 1], r_up.at[step - 1], up).wait_recv()
            up_out[step] += up_in[step - 1]
        start(send_to(up_out.at[step], up_in.at[step], s_up.at[step], r_up.at[step], up))
        t = chunk(2 * step)
        down_out[step] = terms[c, t] + sibling[t]
        if step == 1:
            send_to(down_out.at[0, :, pl.ds(half, half)], down_in.at[0, :, pl.ds(half, half)], s_down.at[0], r_down.at[0], down).wait_recv()
            down_out[step, :, half:] += down_in[0, :, half:]
        else:
            send_to(down_out.at[step - 1], down_in.at[step - 1], s_down.at[step - 1], r_down.at[step - 1], down).wait_recv()
            down_out[step] += down_in[step - 1]
        start(send_to(down_out.at[step], down_in.at[step], s_down.at[step], r_down.at[step], down))
        if step == 1:
            for j in range(1, NY):
                send_to(loss_y.at[0], loss_y.at[j], s_ly.at[j - 1], r_ly.at[j - 1], near[(0, j)]).wait_recv()
            loss_z[0] = jnp.sum(loss_y[...], axis=0)
            for k in range(1, NZ):
                start(send_to(loss_z.at[0], loss_z.at[k], s_lz.at[k - 1], r_lz.at[k - 1], z_peers[k - 1]))
    t = chunk(7)
    send_to(up_out.at[3], up_in.at[3], s_up.at[3], r_up.at[3], up).wait_recv()
    send_to(down_out.at[3], down_in.at[3], s_down.at[3], r_down.at[3], down).wait_recv()
    total = terms[c, t] + sibling[t] + up_in[3] + down_in[3]
    owned[...] = total.reshape(2, NY, OWN, H)
    for n, (dxh, j) in enumerate(YX):
        start(
            send_to(
                owned.at[lax.rem(xh + dxh, 2), lax.rem(y + j, NY)],
                near_in.at[n],
                s_near.at[n],
                r_near.at[n],
                near[(dxh, j)],
            )
        )
    result = owned[xh, y]
    for n, key in enumerate(YX):
        send_to(near_in.at[n], near_in.at[n], s_near.at[n], r_near.at[n], near[key]).wait_recv()
        result = result + near_in[n]
    final[c] = result
    swap = send_to(final.at[c], final.at[c], s_final, r_final, twin)
    swap.start()
    for k in range(1, NZ):
        send_to(loss_z.at[0], loss_z.at[k], s_lz.at[k - 1], r_lz.at[k - 1], z_peers[k - 1]).wait_recv()
    loss_out_ref[...] = jnp.sum(loss_z[...], axis=0)
    send_to(final.at[1 - c], final.at[1 - c], s_final, r_final, twin).wait_recv()
    out_ref[...] = final[...]
    swap.wait_send()
    for copy in copies:
        copy.wait_send()


def reduce_terms(image_terms, text_terms, loss):
    dma = pltpu.SemaphoreType.DMA
    vmem = pl.BlockSpec(memory_space=pltpu.VMEM)
    anywhere = pl.BlockSpec(memory_space=pl.ANY)
    ring = pltpu.VMEM((4, ZROWS, H), F32)
    tile = (8, 128)
    return pl.pallas_call(
        reduce_kernel,
        out_shape=(jax.ShapeDtypeStruct((2, OWN, H), F32), jax.ShapeDtypeStruct((8, 128), F32)),
        in_specs=[anywhere, anywhere, vmem],
        out_specs=(vmem, vmem),
        scratch_shapes=[
            pltpu.VMEM((2, NZ, ZROWS, H), F32),
            pltpu.VMEM((NZ, ZROWS, H), F32),
            ring, ring, ring, ring,
            pltpu.VMEM((2, NY, OWN, H), F32),
            pltpu.VMEM((7, OWN, H), F32),
            pltpu.VMEM((2, OWN, H), F32),
            pltpu.VMEM((8,) + tile, F32),
            pltpu.VMEM((NY,) + tile, F32),
            pltpu.VMEM((NZ,) + tile, F32),
            pltpu.VMEM(tile, F32),
            dma((2, 8)),
            dma((8,)), dma((8,)),
            dma((4,)), dma((4,)),
            dma((4,)), dma((4,)),
            dma((7,)), dma((7,)),
            dma, dma,
            dma((7,)), dma((7,)),
            dma((3,)), dma((3,)),
            dma((7,)), dma((7,)),
        ],
        compiler_params=pltpu.CompilerParams(
            collective_id=2, has_side_effects=True, vmem_limit_bytes=48 * 1024 * 1024
        ),
    )(image_terms.reshape(NZ, ZROWS, H), text_terms.reshape(NZ, ZROWS, H), loss)


def gelu_slope(values):
    return jax.jvp(
        lambda inner: jax.nn.gelu(inner, approximate=True), (values,), (jnp.ones_like(values),)
    )[1]


def tower_block(tokens, weight, offset):
    flat_tokens = tokens.reshape(-1, tokens.shape[2])
    preact = jnp.dot(flat_tokens, weight, preferred_element_type=F32)
    residual = lax.dynamic_slice_in_dim(flat_tokens, offset, weight.shape[1], 1).astype(F32)
    hidden = residual + jax.nn.gelu(preact, approximate=True)
    pooled = jnp.mean(hidden.reshape(tokens.shape[0], tokens.shape[1], -1), axis=1)
    return (flat_tokens, preact, pooled)


def contract_rows(left_rows, right_rows):
    return lax.dot_general(left_rows, right_rows, (((0,), (0,)), ((), ())), preferred_element_type=F32)


def body(
    image_tokens,
    text_tokens,
    image_weight,
    text_weight,
    logit_scale,
    logit_bias,
    loss_scale,
    valid_count,
):
    core = lax.rem(lax.axis_index("dp"), 2)
    half_start = lax.axis_index("mp") * H
    image_flat, image_preact, image_pooled = tower_block(image_tokens, image_weight, half_start)
    text_flat, text_preact, text_pooled = tower_block(text_tokens, text_weight, half_start)
    pooled = jnp.concatenate([image_pooled[:8], text_pooled[:8], image_pooled[8:], text_pooled[8:]], axis=0)
    count = jnp.broadcast_to(valid_count.astype(F32)[:, None], (8, 128))
    grad_pooled, loss_part = pair_gradients(pooled, count, logit_scale, logit_bias, loss_scale)
    grads = grad_pooled.reshape(2, 2, 8, H)
    image_gp = grads[:, 0].reshape(16, H)
    text_gp = grads[:, 1].reshape(16, H)

    def terms(gp, flat, preact, tokens):
        samples, count = tokens.shape[:2]
        slope = gelu_slope(preact.reshape(samples, count, H))
        gpre = (gp[:, None, :] / count * slope).astype(BF16).reshape(-1, H)
        return contract_rows(flat, gpre)

    image_terms = terms(image_gp, image_flat, image_preact, image_tokens)
    text_terms = terms(text_gp, text_flat, text_preact, text_tokens)
    grads_out, loss = reduce_terms(image_terms, text_terms, loss_part)
    mine = lax.dynamic_slice_in_dim(grads_out, core * 12, 12, 1)
    return (loss[0, 0], mine[0], mine[1])


def solution(mesh):
    placed = (
        P("dp", None, None),
        P("dp", None, None),
        P(None, "mp"),
        P(None, "mp"),
        P(),
        P(),
        P(),
        P("dp"),
    )
    return jax.shard_map(
        body,
        mesh=mesh,
        in_specs=placed,
        out_specs=(P(), P("dp", "mp"), P("dp", "mp")),
        check_vma=False,
    )
```

time: 1770 us -> 158 us (0.09)
  waiting for transfers between devices: 1310 us -> 0 us
  blocking collectives: 372 us -> 0 us
  Pallas kernels: 0 us -> 115 us
    unnamed x4 -> x0, waiting for transfers between devices: 969 us -> none
    psum x3 -> x0, blocking collectives: 338 us -> none  [the longest x1 330 us: body(): loss = lax.psum(loss_local / total_count, 'dp')]
    reduce_scatter x1 -> x0, waiting for transfers between devices: 263 us -> none  [body(): lax.psum_scatter(text_terms_of(dlogit, image_bf), 'dp', scatter_dimension...]
    pallas_call x0 -> x2, Pallas kernels: none -> 115 us  [the longest x1 64.1 us: reduce_terms(): pl.pallas_call(reduce_kernel, out_shape=(jax.ShapeDtypeStruct((2, OWN, H)...]
    all_gather x1 -> x0, waiting for transfers between devices: 80.8 us -> none  [body(): all_text = lax.all_gather(text_full, 'dp', axis=0, tiled=True)]
    unnamed x1 -> x0, blocking collectives: 26.7 us -> none
  transfers between devices with their start and end apart: 3 -> 0, of which waited for: 3 -> 0; matrix products, arithmetic and copies ran while one was open for 1% -> 0% of each run, Pallas kernels for 0% -> 0%
where the time goes in v1:
time: 158 us
  Pallas kernels  115 us (73%)
  matrix products  22.4 us (14%)
  local copies, waits for them, and re-layouts  17.3 us (11%)
  between operations  3.32 us (2%)
    pallas_call x1, Pallas kernels, reduce_terms(): pl.pallas_call(reduce_kernel, out_shape=(jax.ShapeDtypeStruct((2, OWN, H)...  64.1 us
    pallas_call x1, Pallas kernels, pair_gradients(): pl.pallas_call(pair_kernel, out_shape=(jax.ShapeDtypeStruct((32, H), F32)...  50.7 us
    dot_general x2, matrix products, contract_rows(): lax.dot_general(left_rows, right_rows, (((0,), (0,)), ((), ())), preferre...  13.3 us
    dot_general x2, local copies, waits for them, and re-layouts, contract_rows(): lax.dot_general(left_rows, right_rows, (((0,), (0,)), ((), ())), preferre...  12.1 us
    dot_general x2, matrix products, tower_block(): preact = jnp.dot(flat_tokens, weight, preferred_element_type=F32)  9.1 us
    unnamed x8, local copies, waits for them, and re-layouts  4 us

profile of v1, /device:TPU:1, one launch (start us, length us, event | category | flops | bytes accessed | tf_op | source)
XLA Modules:
  0.0 157.8 jit_solution(13648713905129040583)
XLA Ops:
  0.6 0.0 copy-start
  0.7 1.6 %copy-done = bf16[1536,768]{1,0:T(8,128)(2,1)S(1)} copy-done((bf16[1536,768]{1,0:T(8,128)(2,1)S(1)}, bf16[1536,768]{1,0:T(8,128)(2,1)}, u32[]{:S(2)}) %copy-start) | copy-done | bytes 2359320
  2.3 0.0 copy-start.2
  2.3 0.0 copy-start.3
  2.3 7.3 %bitcast_reduce_fusion = (f32[16,768]{1,0:T(8,128)S(1)}, f32[1024,768]{1,0:T(8,128)}) fusion(bf16[1024,1536]{1,0:T(8,128)(2,1)} %bitcast.38, s32[]{:T(128)S(6)} %select_n.7, bf16[1536,768]{1,0:T(8,128)(2,1)S(1)} %copy-done), kind=kOutput, calls=%fused_computation.25 | convolution fusion | flops 2424557568 | bytes 10272772 | tf_op jit(solution)/shard_map/dot_general | solution.py:475
  9.6 0.0 copy-done.2
  9.6 0.0 copy-done.3
  9.6 1.8 %bitcast_reduce_fusion.1 = (f32[16,768]{1,0:T(8,128)S(1)}, f32[512,768]{1,0:T(8,128)S(1)}) fusion(bf16[512,1536]{1,0:T(8,128)(2,1)S(1)} %bitcast.39, s32[]{:T(128)S(6)} %select_n.7, bf16[1536,768]{1,0:T(8,128)(2,1)S(1)} %copy-done.2), kind=kOutput, calls=%fused_computation.49 | convolution fusion | flops 1212272640 | bytes 6340612 | tf_op jit(solution)/shard_map/dot_general | solution.py:475
  14.1 50.7 %shard_map.103 = (f32[32,768]{1,0:T(8,128)S(1)}, f32[8,128]{1,0:T(8,128)S(1)}) custom-call(f32[32,768]{1,0:T(8,128)S(1)} %pad_maximum_fusion.pooled_ref, f32[8,128]{1,0:T(8,128)S(1)} %broadcast_in_dim.9.count_ref, f32[1]{0:T(128)S(6)} %copy.13.scale_ref, f32[1]{0:T(128)S(6)} %copy.14.bias_ref, f32[1]{0:T(128)S(6)} %copy.15.loss_scale_ref), custom_call_target="tpu_custom_call" | custom-call | tf_op jit(solution)/shard_map/pallas_call | solution.py:247
  64.8 4.3 %convolution_bitcast_fusion = f32[1536,768]{0,1:T(8,128)} fusion(bf16[16,32,1536]{2,1,0:T(8,128)(2,1)S(1)} %copy-done.3, f32[16,32,768]{2,1,0:T(8,128)S(1)} %bitcast.41, f32[16,768]{1,0:T(8,128)S(1)} %get-tuple-element.13), kind=kOutput, calls=%fused_computation.3 | convolution fusion | flops 1215037440 | bytes 7913472 | tf_op jit(solution)/shard_map/dot_general | solution.py:483
  69.0 6.1 %copy.12 = f32[1536,768]{1,0:T(8,128)} copy(f32[1536,768]{0,1:T(8,128)} %convolution_bitcast_fusion) | data formatting | bytes 9437184 | tf_op jit(solution)/shard_map/dot_general | solution.py:483
  75.1 9.0 %convolution_bitcast_fusion.1 = f32[1536,768]{0,1:T(8,128)} fusion(bf16[16,64,1536]{2,1,0:T(8,128)(2,1)} %param.8, f32[16,64,768]{2,1,0:T(8,128)} %bitcast.40, f32[16,768]{1,0:T(8,128)S(1)} %get-tuple-element.14), kind=kOutput, calls=%fused_computation.4 | convolution fusion | flops 2430074880 | bytes 11059200 | tf_op jit(solution)/shard_map/dot_general | solution.py:483
  84.1 6.1 %copy.11 = f32[1536,768]{1,0:T(8,128)} copy(f32[1536,768]{0,1:T(8,128)} %convolution_bitcast_fusion.1) | data formatting | bytes 9437184 | tf_op jit(solution)/shard_map/dot_general | solution.py:483
  90.2 0.0 copy-start.1
  90.2 2.3 %copy-done.1 = f32[1536,768]{1,0:T(8,128)S(1)} copy-done((f32[1536,768]{1,0:T(8,128)S(1)}, f32[1536,768]{1,0:T(8,128)}, u32[]{:S(2)}) %copy-start.1) | copy-done | bytes 4718616
  92.5 64.1 %shard_map.104 = (f32[2,24,768]{2,1,0:T(8,128)S(1)}, f32[8,128]{1,0:T(8,128)S(1)}) custom-call(f32[8,192,768]{2,1,0:T(8,128)S(1)} %bitcast.35, f32[8,192,768]{2,1,0:T(8,128)} %bitcast.37, f32[8,128]{1,0:T(8,128)S(1)} %get-tuple-element.8.loss_ref), custom_call_target="tpu_custom_call" | custom-call | tf_op jit(solution)/shard_map/pallas_call | solution.py:435
  156.7 0.7 dynamic-slice_bitcast_fusion
  157.3 0.5 slice.33
  (6 shorter events, 0.0 us)
Async XLA Ops:
  0.6 1.7 %copy-start = (bf16[1536,768]{1,0:T(8,128)(2,1)S(1)}, bf16[1536,768]{1,0:T(8,128)(2,1)}, u32[]{:S(2)}) copy-start(bf16[1536,768]{1,0:T(8,128)(2,1)} %param.10) | copy-start | bytes 7077892
  2.3 7.3 %copy-start.2 = (bf16[1536,768]{1,0:T(8,128)(2,1)S(1)}, bf16[1536,768]{1,0:T(8,128)(2,1)}, u32[]{:S(2)}) copy-start(bf16[1536,768]{1,0:T(8,128)(2,1)} %param.11) | copy-start | bytes 7077892
  2.3 7.3 %copy-start.3 = (bf16[16,32,1536]{2,1,0:T(8,128)(2,1)S(1)}, bf16[16,32,1536]{2,1,0:T(8,128)(2,1)}, u32[]{:S(2)}) copy-start(bf16[16,32,1536]{2,1,0:T(8,128)(2,1)} %param.9) | copy-start | bytes 4718596
  90.2 2.3 %copy-start.1 = (f32[1536,768]{1,0:T(8,128)S(1)}, f32[1536,768]{1,0:T(8,128)}, u32[]{:S(2)}) copy-start(f32[1536,768]{1,0:T(8,128)} %copy.11) | copy-start | bytes 14155780

commit v2 on v0

v2 whole, which is shorter than its diff:
```python
import jax
import jax.numpy as jnp
from jax import lax
from jax.experimental import pallas as pl
from jax.experimental.pallas import tpu as pltpu
from jax.sharding import PartitionSpec as P

MESH = pl.DeviceIdType.MESH
F32 = jnp.float32
BF16 = jnp.bfloat16
NZ, NY, NX, NC = 8, 4, 4, 2
D = 1536
H = 768
EXT = 128
ZROWS = D // NZ
OWN = 24


def place():
    dp = lax.axis_index("dp")
    lo = lax.axis_index("mp")
    c = lax.rem(dp, 2)
    y = lax.rem(lax.div(dp, 2), 4)
    xh = lax.rem(lax.div(dp, 8), 2)
    z = lax.div(dp, 16)
    return z, y, xh * 2 + lo, c


def device_at(z, y, x, c):
    return (((z * 2 + lax.div(x, 2)) * 4 + y) * 2 + c, lax.rem(x, 2))


def slot_of(x, c):
    return (lax.div(x, 2) * 2 + c) * 2 + lax.rem(x, 2)


def send_to(src, dst, send_sem, recv_sem, device):
    return pltpu.make_async_remote_copy(
        src_ref=src,
        dst_ref=dst,
        send_sem=send_sem,
        recv_sem=recv_sem,
        device_id=device,
        device_id_type=MESH,
    )


def greet(devices):
    barrier = pltpu.get_barrier_semaphore()
    for device in devices:
        pl.semaphore_signal(barrier, inc=1, device_id=device, device_id_type=MESH)
    pl.semaphore_wait(barrier, len(devices))


GROUP = [(dx, dc) for dx in range(NX) for dc in range(NC) if (dx, dc) != (0, 0)]


def dot_t(a, b):
    return lax.dot_general(a, b, (((1,), (1,)), ((), ())), preferred_element_type=F32)


CODE = 256.0
TOP = 14.98
LEAST = 2.0**-100


def code_of(peak):
    return jnp.ceil(jnp.log2(jnp.maximum(peak, LEAST)) * CODE)


def whole(values):
    return jnp.round(values).astype(jnp.int32)


def encode(values, pad):
    code = code_of(jnp.max(jnp.abs(values), axis=0, keepdims=True))
    digits = whole(values * jnp.exp2(TOP - code / CODE))
    codes = jnp.broadcast_to(code.astype(jnp.int32), (pad, values.shape[1]))
    return jnp.concatenate([digits, codes], axis=0).astype(jnp.int16)


def decode(packed, pad):
    wide = packed.astype(jnp.int32).astype(F32)
    rows = packed.shape[0] - pad
    return wide[:rows] * jnp.exp2(wide[rows : rows + 1] / CODE - TOP)


def slope_of(x):
    k = 0.7978845608028654
    x2 = x * x
    t = jnp.tanh(k * x * (1.0 + 0.044715 * x2))
    return 0.5 * (1.0 + t) + 0.5 * x * (1.0 - t * t) * (k * (1.0 + 3.0 * 0.044715 * x2))


YX = [(dxh, j) for dxh in range(2) for j in range(NY) if (dxh, j) != (0, 0)]
PAIRS = [(0, 1), (2, 0), (2, 1)]
ORDER = [4, 3, 5, 2, 6, 1, 7, 0]
SUBS = 2
SUB = H // SUBS


def kernel(
    pooled_ref,
    count_ref,
    scale_ref,
    bias_ref,
    loss_scale_ref,
    image_ref,
    text_ref,
    image_pre_ref,
    text_pre_ref,
    out_ref,
    loss_out_ref,
    half_out,
    half_in,
    counts,
    plane,
    group,
    parts,
    landed,
    unit_own,
    image_tok,
    text_tok,
    image_t,
    text_t,
    image_pre,
    text_pre,
    image_gpre,
    text_gpre,
    terms,
    sibling,
    up_out,
    up_in,
    down_out,
    down_in,
    near_out,
    near_in,
    final,
    loss_group,
    loss_y,
    loss_z,
    s_load,
    s_other,
    r_other,
    s_count,
    r_count,
    s_group,
    r_group,
    s_y,
    r_y,
    s_up,
    r_up,
    s_down,
    r_down,
    s_part,
    r_part,
    s_sib,
    r_sib,
    s_rup,
    r_rup,
    s_rdown,
    r_rdown,
    s_near,
    r_near,
    s_final,
    r_final,
    s_lg,
    r_lg,
    s_ly,
    r_ly,
    s_lz,
    r_lz,
):
    z, y, x, c = place()
    xh, lo = lax.div(x, 2), lax.rem(x, 2)
    me = slot_of(x, c)
    up = device_at(lax.rem(z + 1, NZ), y, x, c)
    down = device_at(lax.rem(z + NZ - 1, NZ), y, x, c)
    members = {(dx, dc): device_at(z, y, lax.rem(x + dx, NX), lax.rem(c + dc, NC)) for dx, dc in GROUP}
    sources = {(dx, dc): (lax.rem(x + NX - dx, NX), lax.rem(c + dc, NC)) for dx, dc in GROUP}
    near = {(dxh, j): device_at(z, lax.rem(y + j, NY), lax.rem(xh + dxh, 2) * 2 + lo, c) for dxh, j in YX}
    y_peers = [near[(0, j)] for j in range(1, NY)]
    z_peers = [device_at(lax.rem(z + k, NZ), y, x, c) for k in range(1, NZ)]
    partner = device_at(z, y, xh * 2 + 1 - lo, c)
    twin = members[(0, 1)]
    copies = []

    def start(*args):
        copy = send_to(*args)
        copy.start()
        copies.append(copy)

    loads = [
        pltpu.make_async_copy(src, dst, s_load.at[n])
        for n, (src, dst) in enumerate(
            [(image_ref, image_tok), (text_ref, text_tok), (image_pre_ref, image_pre), (text_pre_ref, text_pre)]
        )
    ]
    for load in loads:
        load.start()
    greet([members[key] for key in GROUP] + [near[key] for key in YX if key != (1, 0)] + z_peers)

    mine = pooled_ref[...]
    first = lo == 0
    own_sq = jnp.sum(mine * mine, axis=1, keepdims=True)
    half_out[:, :H] = jnp.where(first, mine[16:32], mine[0:16])
    half_out[:, H:] = jnp.broadcast_to(jnp.where(first, own_sq[0:16], own_sq[16:32]), (16, EXT))
    start(half_out, half_in, s_other, r_other, partner)
    pair_slot = xh * 2 + c
    counts[pair_slot] = count_ref[...]
    for n, key in enumerate(PAIRS):
        start(counts.at[pair_slot], counts.at[pair_slot], s_count.at[n], r_count.at[n], members[key])
    own_rows = jnp.where(first, mine[0:16], mine[16:32])
    own_rows_sq = jnp.where(first, own_sq[0:16], own_sq[16:32])
    rest_sq = jnp.where(first, own_sq[16:32], own_sq[0:16])
    send_to(half_out, half_in, s_other, r_other, partner).wait_recv()
    theirs = half_in[:, :H]
    norm_own = jnp.sqrt(own_rows_sq + jnp.sum(theirs * theirs, axis=1, keepdims=True) + 1e-6)
    norm_rest = jnp.sqrt(rest_sq + half_in[:, H : H + 1] + 1e-6)
    norm = jnp.concatenate(
        [jnp.where(first, norm_own, norm_rest), jnp.where(first, norm_rest, norm_own)], axis=0
    )
    unit_own[...] = mine / norm
    unit_mine = own_rows / norm_own
    unit_theirs = theirs / norm_own
    low = jnp.where(first, unit_mine, unit_theirs)
    high = jnp.where(first, unit_theirs, unit_mine)
    for n, (dx, dc) in enumerate(PAIRS):
        slot = lax.rem(xh + dx // 2, 2) * 2 + lax.rem(c + dc, NC)
        send_to(counts.at[slot], counts.at[slot], s_count.at[n], r_count.at[n], members[(dx, dc)]).wait_recv()
    row_total = jnp.sum(counts[...], axis=0)[0:1, :]
    own_count = count_ref[0:1, :]
    sample = lax.rem(lax.broadcasted_iota(jnp.int32, (16, EXT), 0), 8) + 8 * lo
    lane = lax.broadcasted_iota(jnp.int32, (16, EXT), 1)
    usable = jnp.where(sample.astype(F32) < own_count, 1.0, 0.0)
    extra = jnp.where(lane < EXT // 2, usable, jnp.broadcast_to(row_total, (16, EXT)))
    block = jnp.concatenate([low.astype(BF16), high.astype(BF16), extra.astype(BF16)], axis=1)
    plane[z, y] = block
    group[me] = block

    def pass_up(step, j, zs, ys):
        start(plane.at[zs, ys], plane.at[zs, ys], s_up.at[step, j], r_up.at[step, j], up)

    def pass_down(step, j, zs, ys):
        start(plane.at[zs, ys], plane.at[zs, ys], s_down.at[step, j], r_down.at[step, j], down)

    for j in range(1, NY):
        start(plane.at[z, y], plane.at[z, y], s_y.at[j - 1], r_y.at[j - 1], y_peers[j - 1])
    pass_up(0, 0, z, y)
    pass_down(0, 0, z, y)
    for n, key in enumerate(GROUP):
        start(group.at[me], group.at[me], s_group.at[n], r_group.at[n], members[key])

    def turn(tok, out, p):
        def work():
            flipped = tok[:, 384 * p : 384 * p + 384].T
            out[2 * p : 2 * p + 2] = flipped.reshape(2, ZROWS, tok.shape[0])

        return work

    def bend(pre, first_row, rows):
        def work():
            @pl.loop(0, rows // 16)
            def _(i):
                at = pl.ds(pl.multiple_of(first_row + i * 16, 16), 16)
                pre[at, :] = slope_of(pre[at, :])

        return work

    for load in loads:
        load.wait()
    pieces = [turn(image_tok, image_t, p) for p in range(4)] + [turn(text_tok, text_t, p) for p in range(4)]
    pieces += [bend(image_pre, 128 * p, 128) for p in range(8)] + [bend(text_pre, 128 * p, 128) for p in range(4)]
    done = [0]

    def idle(amount=1):
        for piece in pieces[done[0] : done[0] + amount]:
            piece()
        done[0] += amount

    for j in range(1, NY):
        ys = lax.rem(y + NY - j, NY)
        send_to(plane.at[z, ys], plane.at[z, ys], s_y.at[j - 1], r_y.at[j - 1], up).wait_recv()
        pass_up(0, j, z, ys)
        pass_down(0, j, z, ys)
    idle()
    for step in range(4):
        for j in range(NY):
            ys = lax.rem(y + NY - j, NY)
            if step < 3 or j < 2:
                zs = lax.rem(z + NZ - step - 1, NZ)
                send_to(plane.at[zs, ys], plane.at[zs, ys], s_up.at[step, j], r_up.at[step, j], up).wait_recv()
                if step < 2 or (step == 2 and j < 2):
                    pass_up(step + 1, j, zs, ys)
            if step < 3 or j >= 2:
                zs = lax.rem(z + step + 1, NZ)
                send_to(plane.at[zs, ys], plane.at[zs, ys], s_down.at[step, j], r_down.at[step, j], down).wait_recv()
                if step < 2 or (step == 2 and j >= 2):
                    pass_down(step + 1, j, zs, ys)
            idle(2 if step < 1 else 1)
    idle(len(pieces) - done[0])
    for n, key in enumerate(GROUP):
        slot = slot_of(*sources[key])
        send_to(group.at[slot], group.at[slot], s_group.at[n], r_group.at[n], members[key]).wait_recv()

    rows = group[...].reshape(8 * 16, D + EXT)
    cols = plane[...].reshape(32 * 16, D + EXT)
    row_main, col_main = rows[:, :D], cols[:, :D]
    logit_mult = scale_ref[0]
    logits = logit_mult * dot_t(row_main, col_main) + bias_ref[0]
    pick = lax.broadcasted_iota(jnp.int32, (16, EXT), 0) * (EXT // 2)
    pick = jnp.where(pick == lax.broadcasted_iota(jnp.int32, (16, EXT), 1), 1.0, 0.0).astype(BF16)
    col_extra = dot_t(pick, cols[:, D:])
    total = jnp.sum(col_extra[1:2, :]) * (1.0 / 16.0)
    col_usable = col_extra[0:1, :]
    row_usable = rows[:, D : D + 1].astype(F32)
    shape = (8 * 16, 32 * 16)
    r = lax.broadcasted_iota(jnp.int32, shape, 0)
    q = lax.broadcasted_iota(jnp.int32, shape, 1)
    r_text = lax.rem(lax.div(r, 8), 2)
    q_text = lax.rem(lax.div(q, 8), 2)
    same = (lax.div(r, 16) == me) & (lax.div(q, 16) == z * NY + y) & (lax.rem(r, 8) == lax.rem(q, 8))
    used = (row_usable * col_usable > 0.5) & (r_text != q_text)
    sign = jnp.where(same, 1.0, -1.0)
    margin = -sign * logits
    coeff = loss_scale_ref[0] / total
    dlogit = (jnp.where(used, -sign * jax.nn.sigmoid(margin), 0.0) * coeff).astype(BF16)
    grad = logit_mult * jnp.dot(dlogit, col_main, preferred_element_type=F32)
    radial = jnp.sum(row_main.astype(F32) * grad, axis=1, keepdims=True)
    code = code_of(jnp.max(jnp.abs(grad), axis=1, keepdims=True))
    factor = jnp.exp2(TOP - code / CODE)
    digits = whole(grad * factor).astype(jnp.int16)
    radial = whole(radial * factor * (1.0 / 40.0))
    side = lax.broadcasted_iota(jnp.int32, (8 * 16, EXT), 1) < EXT // 2
    side = jnp.where(side, code.astype(jnp.int32), radial).astype(jnp.int16)
    for pair in range(4):
        for half in range(2):
            band = slice(pair * 32, pair * 32 + 32)
            parts[pair, half, :, :H] = digits[band, half * H : half * H + H]
            parts[pair, half, :, H:] = side[band]

    for n, (dx, dc) in enumerate(GROUP):
        tx, tc = lax.rem(x + dx, NX), lax.rem(c + dc, NC)
        src = parts.at[lax.div(tx, 2) * 2 + tc, lax.rem(tx, 2)]
        start(src, landed.at[me], s_part.at[n], r_part.at[n], members[(dx, dc)])

    soft = jnp.maximum(margin, 0.0) + jnp.log1p(jnp.exp(-jnp.abs(margin)))
    loss = jnp.sum(jnp.where(used & (r_text == 0), soft, 0.0), axis=1, keepdims=True)
    loss_group[0] = jnp.broadcast_to(jnp.sum(loss, axis=0, keepdims=True) / total, (8, 128))
    for n, key in enumerate(GROUP):
        start(loss_group.at[0], loss_group.at[n + 1], s_lg.at[n], r_lg.at[n], members[key])

    def opened(packed):
        wide = packed.astype(jnp.int32).astype(F32)
        back = jnp.exp2(wide[:, H : H + 1] / CODE - TOP)
        return wide[:, :H] * back, wide[:, H + EXT // 2 : H + EXT // 2 + 1] * (back * 40.0)

    sum_grad, sum_radial = opened(parts[pair_slot, lo])
    for n, key in enumerate(GROUP):
        slot = slot_of(*sources[key])
        send_to(landed.at[slot], landed.at[slot], s_part.at[n], r_part.at[n], members[key]).wait_recv()
        more_grad, more_radial = opened(landed[slot])
        sum_grad = sum_grad + more_grad
        sum_radial = sum_radial + more_radial
    gp = (sum_grad - unit_own[...] * sum_radial) / norm
    for i in range(16):
        row = (i // 8) * 16 + i % 8
        at = slice(64 * i, 64 * i + 64)
        image_gpre[at, :] = (gp[row : row + 1] / 64.0 * image_pre[at, :]).astype(BF16)
        at = slice(32 * i, 32 * i + 32)
        text_gpre[at, :] = (gp[row + 8 : row + 9] / 32.0 * text_pre[at, :]).astype(BF16)

    def compute(n):
        t = lax.rem(z + ORDER[n], NZ)
        terms[0, t] = jnp.dot(image_t[t], image_gpre[...], preferred_element_type=F32)
        terms[1, t] = jnp.dot(text_t[t], text_gpre[...], preferred_element_type=F32)
        start(terms.at[1 - c, t], sibling.at[t], s_sib.at[n], r_sib.at[n], twin)

    def chunk(n):
        t = lax.rem(z + ORDER[n], NZ)
        send_to(sibling.at[t], sibling.at[t], s_sib.at[n], r_sib.at[n], twin).wait_recv()
        return t

    def ring(step, n, out, inn, send_sem, recv_sem, way, split):
        t = chunk(n) if n is not None else lax.rem(z + ORDER[0], NZ)
        for h in range(SUBS):
            if step == 0 and h != split:
                continue
            at = slice(h * SUB, h * SUB + SUB)
            value = terms[c, t, :, at] + sibling[t, :, at]
            if step > 1 or (step == 1 and h == split):
                send_to(out.at[step - 1, h], inn.at[step - 1, h], send_sem.at[step - 1, h], recv_sem.at[step - 1, h], way).wait_recv()
                value = value + decode(inn[step - 1, h], 16)
            out[step, h] = encode(value, 16)
            start(out.at[step, h], inn.at[step, h], send_sem.at[step, h], recv_sem.at[step, h], way)

    def ring_up(step, n):
        ring(step, n, up_out, up_in, s_rup, r_rup, up, 0)

    def ring_down(step, n):
        ring(step, n, down_out, down_in, s_rdown, r_rdown, down, 1)

    compute(0)
    compute(1)
    ring_up(0, 0)
    ring_down(0, None)
    compute(2)
    compute(3)
    for n, key in enumerate(GROUP):
        send_to(loss_group.at[0], loss_group.at[n + 1], s_lg.at[n], r_lg.at[n], members[key]).wait_recv()
    loss_y[0] = jnp.sum(loss_group[...], axis=0)
    for j in range(1, NY):
        start(loss_y.at[0], loss_y.at[j], s_ly.at[j - 1], r_ly.at[j - 1], y_peers[j - 1])
    ring_up(1, 1)
    ring_down(1, 2)
    compute(4)
    compute(5)
    for j in range(1, NY):
        send_to(loss_y.at[0], loss_y.at[j], s_ly.at[j - 1], r_ly.at[j - 1], y_peers[j - 1]).wait_recv()
    loss_z[0] = jnp.sum(loss_y[...], axis=0)
    for k in range(1, NZ):
        start(loss_z.at[0], loss_z.at[k], s_lz.at[k - 1], r_lz.at[k - 1], z_peers[k - 1])
    ring_up(2, 3)
    ring_down(2, 4)
    compute(6)
    compute(7)
    ring_up(3, 5)
    ring_down(3, 6)
    for k in range(1, NZ):
        send_to(loss_z.at[0], loss_z.at[k], s_lz.at[k - 1], r_lz.at[k - 1], z_peers[k - 1]).wait_recv()
    loss_out_ref[...] = jnp.sum(loss_z[...], axis=0)
    t = chunk(7)
    own = []
    for h in range(SUBS):
        at = slice(h * SUB, h * SUB + SUB)
        value = terms[c, t, :, at] + sibling[t, :, at]
        send_to(up_out.at[3, h], up_in.at[3, h], s_rup.at[3, h], r_rup.at[3, h], up).wait_recv()
        value = value + decode(up_in[3, h], 16)
        send_to(down_out.at[3, h], down_in.at[3, h], s_rdown.at[3, h], r_rdown.at[3, h], down).wait_recv()
        own.append(value + decode(down_in[3, h], 16))
    own = jnp.concatenate(own, axis=1).reshape(2 * NY, OWN, H)
    for i in range(2 * NY):
        near_out[i] = encode(own[i], 8)
    for n, (dxh, j) in enumerate(YX):
        src = near_out.at[lax.rem(xh + dxh, 2) * NY + lax.rem(y + j, NY)]
        start(src, near_in.at[n], s_near.at[n], r_near.at[n], near[(dxh, j)])
    result = decode(near_out[xh * NY + y], 8)
    for n, key in enumerate(YX):
        send_to(near_in.at[n], near_in.at[n], s_near.at[n], r_near.at[n], near[key]).wait_recv()
        result = result + decode(near_in[n], 8)
    final[c] = result
    start(final.at[c], final.at[c], s_final, r_final, twin)
    send_to(final.at[1 - c], final.at[1 - c], s_final, r_final, twin).wait_recv()
    out_ref[...] = final[...]
    for copy in copies:
        copy.wait_send()


def run_kernel(pooled, count, logit_scale, logit_bias, loss_scale, image, text, image_pre, text_pre):
    dma = pltpu.SemaphoreType.DMA
    vmem = pl.BlockSpec(memory_space=pltpu.VMEM)
    smem = pl.BlockSpec(memory_space=pltpu.SMEM)
    anywhere = pl.BlockSpec(memory_space=pl.ANY)
    image_rows, text_rows = image.shape[0], text.shape[0]
    ring = pltpu.VMEM((4, SUBS, ZROWS + 16, SUB), jnp.int16)
    tile = (8, 128)
    return pl.pallas_call(
        kernel,
        out_shape=(jax.ShapeDtypeStruct((2, OWN, H), F32), jax.ShapeDtypeStruct(tile, F32)),
        in_specs=[vmem, vmem, smem, smem, smem, anywhere, anywhere, anywhere, anywhere],
        out_specs=(vmem, vmem),
        scratch_shapes=[
            pltpu.VMEM((16, H + EXT), F32),
            pltpu.VMEM((16, H + EXT), F32),
            pltpu.VMEM((4,) + tile, F32),
            pltpu.VMEM((NZ, NY, 16, D + EXT), BF16),
            pltpu.VMEM((8, 16, D + EXT), BF16),
            pltpu.VMEM((4, 2, 32, H + EXT), jnp.int16),
            pltpu.VMEM((8, 32, H + EXT), jnp.int16),
            pltpu.VMEM((32, H), F32),
            pltpu.VMEM((image_rows, D), BF16),
            pltpu.VMEM((text_rows, D), BF16),
            pltpu.VMEM((NZ, ZROWS, image_rows), BF16),
            pltpu.VMEM((NZ, ZROWS, text_rows), BF16),
            pltpu.VMEM((image_rows, H), F32),
            pltpu.VMEM((text_rows, H), F32),
            pltpu.VMEM((image_rows, H), BF16),
            pltpu.VMEM((text_rows, H), BF16),
            pltpu.VMEM((2, NZ, ZROWS, H), F32),
            pltpu.VMEM((NZ, ZROWS, H), F32),
            ring,
            ring,
            ring,
            ring,
            pltpu.VMEM((2 * NY, 32, H), jnp.int16),
            pltpu.VMEM((7, 32, H), jnp.int16),
            pltpu.VMEM((2, OWN, H), F32),
            pltpu.VMEM((8,) + tile, F32),
            pltpu.VMEM((NY,) + tile, F32),
            pltpu.VMEM((NZ,) + tile, F32),
            dma((4,)),
        ]
        + [dma] * 2
        + [dma((3,))] * 2
        + [dma((7,))] * 2
        + [dma((3,))] * 2
        + [dma((4, 4))] * 4
        + [dma((7,))] * 2
        + [dma((8,))] * 2
        + [dma((4, SUBS))] * 4
        + [dma((7,))] * 2
        + [dma] * 2
        + [dma((7,))] * 2
        + [dma((3,))] * 2
        + [dma((7,))] * 2,
        compiler_params=pltpu.CompilerParams(
            collective_id=1, has_side_effects=True, vmem_limit_bytes=58 * 1024 * 1024
        ),
    )(pooled, count, logit_scale, logit_bias, loss_scale, image, text, image_pre, text_pre)


def tower_block(tokens, weight, offset):
    flat_tokens = tokens.reshape(-1, tokens.shape[2])
    preact = jnp.dot(flat_tokens, weight, preferred_element_type=F32)
    residual = lax.dynamic_slice_in_dim(flat_tokens, offset, weight.shape[1], 1).astype(F32)
    hidden = residual + jax.nn.gelu(preact, approximate=True)
    pooled = jnp.mean(hidden.reshape(tokens.shape[0], tokens.shape[1], -1), axis=1)
    return (flat_tokens, preact, pooled)


def body(
    image_tokens,
    text_tokens,
    image_weight,
    text_weight,
    logit_scale,
    logit_bias,
    loss_scale,
    valid_count,
):
    core = lax.rem(lax.axis_index("dp"), 2)
    half_start = lax.axis_index("mp") * H
    image_flat, image_preact, image_pooled = tower_block(image_tokens, image_weight, half_start)
    text_flat, text_preact, text_pooled = tower_block(text_tokens, text_weight, half_start)
    pooled = jnp.concatenate([image_pooled[:8], text_pooled[:8], image_pooled[8:], text_pooled[8:]], axis=0)
    count = jnp.broadcast_to(valid_count.astype(F32)[:, None], (8, 128))
    grads_out, loss = run_kernel(
        pooled, count, logit_scale, logit_bias, loss_scale, image_flat, text_flat, image_preact, text_preact
    )
    mine = lax.dynamic_slice_in_dim(grads_out, core * 12, 12, 1)
    return (loss[0, 0], mine[0], mine[1])


def solution(mesh):
    placed = (
        P("dp", None, None),
        P("dp", None, None),
        P(None, "mp"),
        P(None, "mp"),
        P(),
        P(),
        P(),
        P("dp"),
    )
    return jax.shard_map(
        body,
        mesh=mesh,
        in_specs=placed,
        out_specs=(P(), P("dp", "mp"), P("dp", "mp")),
        check_vma=False,
    )
```

time: 1770 us -> 108 us (0.06)
  waiting for transfers between devices: 1310 us -> 0 us
  blocking collectives: 372 us -> 0 us
  Pallas kernels: 0 us -> 88.6 us
  matrix products: 35 us -> 10.2 us
    unnamed x4 -> x0, waiting for transfers between devices: 969 us -> none
    psum x3 -> x0, blocking collectives: 338 us -> none  [the longest x1 330 us: body(): loss = lax.psum(loss_local / total_count, 'dp')]
    reduce_scatter x1 -> x0, waiting for transfers between devices: 263 us -> none  [body(): lax.psum_scatter(text_terms_of(dlogit, image_bf), 'dp', scatter_dimension...]
    pallas_call x0 -> x1, Pallas kernels: none -> 88.6 us  [run_kernel(): pl.pallas_call(kernel, out_shape=(jax.ShapeDtypeStruct((2, OWN, H), F32),...]
    all_gather x1 -> x0, waiting for transfers between devices: 80.8 us -> none  [body(): all_text = lax.all_gather(text_full, 'dp', axis=0, tiled=True)]
    unnamed x1 -> x0, blocking collectives: 26.7 us -> none
    dot_general x7 -> x2, matrix products: 35 us -> 10.2 us  [tower_block(): preact = jnp.dot(flat_tokens, weight, preferred_element_type=F32)]
  transfers between devices with their start and end apart: 3 -> 0, of which waited for: 3 -> 0; matrix products, arithmetic and copies ran while one was open for 1% -> 0% of each run, Pallas kernels for 0% -> 0%
where the time goes in v2:
time: 108 us
  Pallas kernels  88.6 us (82%)
  matrix products  10.2 us (9%)
  local copies, waits for them, and re-layouts  4.94 us (5%)
  between operations  3.28 us (3%)
    pallas_call x1, Pallas kernels, run_kernel(): pl.pallas_call(kernel, out_shape=(jax.ShapeDtypeStruct((2, OWN, H), F32),...  88.6 us
    dot_general x2, matrix products, tower_block(): preact = jnp.dot(flat_tokens, weight, preferred_element_type=F32)  10.2 us

profile of v2, /device:TPU:1, one launch (start us, length us, event | category | flops | bytes accessed | tf_op | source)
XLA Modules:
  0.0 107.7 jit_solution(8402277112895600715)
XLA Ops:
  0.6 0.0 copy-start
  0.7 1.6 %copy-done = bf16[1536,768]{1,0:T(8,128)(2,1)S(1)} copy-done((bf16[1536,768]{1,0:T(8,128)(2,1)S(1)}, bf16[1536,768]{1,0:T(8,128)(2,1)}, u32[]{:S(2)}) %copy-start) | copy-done | bytes 2359320
  2.3 0.0 copy-start.1
  2.3 0.0 copy-start.2
  2.3 7.3 %bitcast_reduce_fusion = (f32[16,768]{1,0:T(8,128)S(1)}, f32[1024,768]{1,0:T(8,128)}) fusion(bf16[1024,1536]{1,0:T(8,128)(2,1)} %bitcast.16, s32[]{:T(128)S(6)} %select_n.7, bf16[1536,768]{1,0:T(8,128)(2,1)S(1)} %copy-done), kind=kOutput, calls=%fused_computation.9 | convolution fusion | flops 2424557568 | bytes 10272772 | tf_op jit(solution)/shard_map/dot_general | solution.py:524
  9.6 0.0 copy-done.1
  9.6 0.0 copy-done.2
  9.7 2.9 %bitcast_reduce_fusion.1 = (f32[16,768]{1,0:T(8,128)S(1)}, f32[512,768]{1,0:T(8,128)}) fusion(bf16[512,1536]{1,0:T(8,128)(2,1)S(1)} %bitcast.19, s32[]{:T(128)S(6)} %select_n.7, bf16[1536,768]{1,0:T(8,128)(2,1)S(1)} %copy-done.2), kind=kOutput, calls=%fused_computation.19 | convolution fusion | flops 1212272640 | bytes 6340612 | tf_op jit(solution)/shard_map/dot_general | solution.py:524
  12.5 0.6 pad_maximum_fusion.pooled_ref
  13.8 0.6 broadcast_in_dim.9.count_ref
  16.4 88.6 %shard_map.103 = (f32[2,24,768]{2,1,0:T(8,128)}, f32[8,128]{1,0:T(8,128)}) custom-call(f32[32,768]{1,0:T(8,128)} %pad_maximum_fusion.pooled_ref, f32[8,128]{1,0:T(8,128)} %broadcast_in_dim.9.count_ref, f32[1]{0:T(128)S(6)} %copy.11.scale_ref, f32[1]{0:T(128)S(6)} %copy.12.bias_ref, f32[1]{0:T(128)S(6)} %copy.13.loss_scale_ref, bf16[1024,1536]{1,0:T(8,128)(2,1)} %bitcast.17, ...), custom_call_target="tpu_custom_call" | custom-call | tf_op jit(solution)/shard_map/pallas_call | solution.py:467
  105.0 1.5 %dynamic-slice_bitcast_fusion = (f32[12,768]{1,0:T(8,128)}, f32[12,768]{1,0:T(8,128)}) fusion(f32[2,24,768]{2,1,0:T(8,128)} %get-tuple-element.6, s32[]{:T(128)S(6)} %add.41, s32[]{:T(128)S(6)} %select_n.8), kind=kLoop, calls=%fused_computation.21 | loop fusion | bytes 147464 | tf_op jit(solution)/shard_map/squeeze | solution.py:551
  106.5 1.2 %slice.25 = f32[1,1]{1,0:T(1,128)} slice(f32[8,128]{1,0:T(8,128)} %get-tuple-element.5), slice={[0:1], [0:1]} | slice | bytes 8 | tf_op jit(solution)/shard_map/slice | solution.py:551
  (3 shorter events, 0.0 us)
Async XLA Ops:
  0.6 1.7 %copy-start = (bf16[1536,768]{1,0:T(8,128)(2,1)S(1)}, bf16[1536,768]{1,0:T(8,128)(2,1)}, u32[]{:S(2)}) copy-start(bf16[1536,768]{1,0:T(8,128)(2,1)} %param.10) | copy-start | bytes 7077892
  2.3 7.3 %copy-start.1 = (bf16[16,32,1536]{2,1,0:T(8,128)(2,1)S(1)}, bf16[16,32,1536]{2,1,0:T(8,128)(2,1)}, u32[]{:S(2)}) copy-start(bf16[16,32,1536]{2,1,0:T(8,128)(2,1)} %param.9) | copy-start | bytes 4718596
  2.3 7.3 %copy-start.2 = (bf16[1536,768]{1,0:T(8,128)(2,1)S(1)}, bf16[1536,768]{1,0:T(8,128)(2,1)}, u32[]{:S(2)}) copy-start(bf16[1536,768]{1,0:T(8,128)(2,1)} %param.11) | copy-start | bytes 7077892

commit v3 on v2

--- a/solution.py
+++ b/solution.py
@@ -85,6 +85,11 @@
     return wide[:rows] * jnp.exp2(wide[rows : rows + 1] / CODE - TOP)
 
 
+def gelu(x):
+    k = 0.7978845608028654
+    return 0.5 * x * (1.0 + jnp.tanh(k * x * (1.0 + 0.044715 * (x * x))))
+
+
 def slope_of(x):
     k = 0.7978845608028654
     x2 = x * x
@@ -96,21 +101,26 @@
 PAIRS = [(0, 1), (2, 0), (2, 1)]
 ORDER = [4, 3, 5, 2, 6, 1, 7, 0]
 SUBS = 2
-SUB = H // SUBS
+SUB = 256
+FAR = SUBS * SUB
+REST = H - FAR
 
 
 def kernel(
-    pooled_ref,
     count_ref,
     scale_ref,
     bias_ref,
     loss_scale_ref,
     image_ref,
     text_ref,
-    image_pre_ref,
-    text_pre_ref,
-    out_ref,
+    image_weight_ref,
+    text_weight_ref,
+    image_out_ref,
+    text_out_ref,
     loss_out_ref,
+    image_weight,
+    text_weight,
+    pooled,
     half_out,
     half_in,
     counts,
@@ -135,6 +145,11 @@
     down_in,
     near_out,
     near_in,
+    wide_out,
+    wide_in,
+    line_out,
+    line_in,
+    rest_own,
     final,
     loss_group,
     loss_y,
@@ -162,6 +177,10 @@
     r_rdown,
     s_near,
     r_near,
+    s_wide,
+    r_wide,
+    s_line,
+    r_line,
     s_final,
     r_final,
     s_lg,
@@ -190,33 +209,82 @@
         copy.start()
         copies.append(copy)
 
-    loads = [
-        pltpu.make_async_copy(src, dst, s_load.at[n])
-        for n, (src, dst) in enumerate(
-            [(image_ref, image_tok), (text_ref, text_tok), (image_pre_ref, image_pre), (text_pre_ref, text_pre)]
-        )
-    ]
-    for load in loads:
-        load.start()
-    greet([members[key] for key in GROUP] + [near[key] for key in YX if key != (1, 0)] + z_peers)
-
-    mine = pooled_ref[...]
+    loads = {}
+
+    def fetch(name, src, dst):
+        loads[name] = pltpu.make_async_copy(src, dst, s_load.at[len(loads)])
+        loads[name].start()
+
+    fetch("tw", text_weight_ref, text_weight)
+    for p in range(2):
+        at = pl.ds(256 * p, 256)
+        fetch("t%d" % p, text_ref.at[at], text_tok.at[at])
+    fetch("iw", image_weight_ref, image_weight)
+    for p in range(4):
+        at = pl.ds(256 * p, 256)
+        fetch("i%d" % p, image_ref.at[at], image_tok.at[at])
+    peers = [members[key] for key in GROUP] + [near[key] for key in YX if key != (1, 0)] + z_peers
+    barrier = pltpu.get_barrier_semaphore()
+    for peer in peers:
+        pl.semaphore_signal(barrier, inc=1, device_id=peer, device_id_type=MESH)
+
+    columns = pl.ds(pl.multiple_of(lo * H, H), H)
+
+    def forward(tok, weight, pre, p):
+        at = slice(256 * p, 256 * p + 256)
+        pre[at, :] = jnp.dot(tok[at, :], weight[...], preferred_element_type=F32)
+
+    def pool(tok, pre, p, tokens, offset):
+        for i in range(256 // tokens):
+            at = slice(256 * p + tokens * i, 256 * p + tokens * i + tokens)
+            hidden = tok[at, columns].astype(F32) + gelu(pre[at, :])
+            sample = 256 // tokens * p + i
+            row = (sample // 8) * 16 + offset + sample % 8
+            pooled[row : row + 1, :] = jnp.sum(hidden, axis=0, keepdims=True) * (1.0 / tokens)
+
     first = lo == 0
-    own_sq = jnp.sum(mine * mine, axis=1, keepdims=True)
-    half_out[:, :H] = jnp.where(first, mine[16:32], mine[0:16])
-    half_out[:, H:] = jnp.broadcast_to(jnp.where(first, own_sq[0:16], own_sq[16:32]), (16, EXT))
-    start(half_out, half_in, s_other, r_other, partner)
     pair_slot = xh * 2 + c
+
+    def swap(w):
+        low, high = pooled[8 * w : 8 * w + 8, :], pooled[16 + 8 * w : 24 + 8 * w, :]
+        ours = jnp.where(first, low, high)
+        squares = jnp.sum(ours * ours, axis=1, keepdims=True)
+        half_out[w, :, :H] = jnp.where(first, high, low)
+        half_out[w, :, H:] = jnp.broadcast_to(squares, (8, EXT))
+        start(half_out.at[w], half_in.at[w], s_other.at[w], r_other.at[w], partner)
+
+    for name in ("tw", "t0"):
+        loads[name].wait()
+    forward(text_tok, text_weight, text_pre, 0)
+    loads["t1"].wait()
+    forward(text_tok, text_weight, text_pre, 1)
+    pool(text_tok, text_pre, 0, 32, 8)
+    for name in ("iw", "i0"):
+        loads[name].wait()
+    forward(image_tok, image_weight, image_pre, 0)
+    pool(text_tok, text_pre, 1, 32, 8)
+    pl.semaphore_wait(barrier, len(peers))
+    swap(1)
     counts[pair_slot] = count_ref[...]
     for n, key in enumerate(PAIRS):
         start(counts.at[pair_slot], counts.at[pair_slot], s_count.at[n], r_count.at[n], members[key])
+    for p in range(1, 4):
+        loads["i%d" % p].wait()
+        forward(image_tok, image_weight, image_pre, p)
+        pool(image_tok, image_pre, p - 1, 64, 0)
+    pool(image_tok, image_pre, 3, 64, 0)
+    swap(0)
+    mine = pooled[...]
+    own_sq = jnp.sum(mine * mine, axis=1, keepdims=True)
     own_rows = jnp.where(first, mine[0:16], mine[16:32])
     own_rows_sq = jnp.where(first, own_sq[0:16], own_sq[16:32])
     rest_sq = jnp.where(first, own_sq[16:32], own_sq[0:16])
-    send_to(half_out, half_in, s_other, r_other, partner).wait_recv()
-    theirs = half_in[:, :H]
+    for w in range(2):
+        send_to(half_out.at[w], half_in.at[w], s_other.at[w], r_other.at[w], partner).wait_recv()
+    arrived = half_in[...].reshape(16, H + EXT)
+    theirs = arrived[:, :H]
     norm_own = jnp.sqrt(own_rows_sq + jnp.sum(theirs * theirs, axis=1, keepdims=True) + 1e-6)
-    norm_rest = jnp.sqrt(rest_sq + half_in[:, H : H + 1] + 1e-6)
+    norm_rest = jnp.sqrt(rest_sq + arrived[:, H : H + 1] + 1e-6)
     norm = jnp.concatenate(
         [jnp.where(first, norm_own, norm_rest), jnp.where(first, norm_rest, norm_own)], axis=0
     )
@@ -267,8 +335,6 @@
 
         return work
 
-    for load in loads:
-        load.wait()
     pieces = [turn(image_tok, image_t, p) for p in range(4)] + [turn(text_tok, text_t, p) for p in range(4)]
     pieces += [bend(image_pre, 128 * p, 128) for p in range(8)] + [bend(text_pre, 128 * p, 128) for p in range(4)]
     done = [0]
@@ -382,7 +448,7 @@
         return t
 
     def ring(step, n, out, inn, send_sem, recv_sem, way, split):
-        t = chunk(n) if n is not None else lax.rem(z + ORDER[0], NZ)
+        t = lax.rem(z + ORDER[n], NZ)
         for h in range(SUBS):
             if step == 0 and h != split:
                 continue
@@ -400,10 +466,36 @@
     def ring_down(step, n):
         ring(step, n, down_out, down_in, s_rdown, r_rdown, down, 1)
 
+    def spread(q):
+        values = []
+        for n in range(4 * q, 4 * q + 4):
+            t = lax.rem(z + ORDER[n], NZ)
+            values.append((terms[c, t, :, FAR:] + sibling[t, :, FAR:]).reshape(2 * NY, OWN, REST))
+        for i in range(2 * NY):
+            wide_out[q, i] = encode(jnp.concatenate([value[i] for value in values], axis=0), 16)
+        for n, (dxh, j) in enumerate(YX):
+            src = wide_out.at[q, lax.rem(xh + dxh, 2) * NY + lax.rem(y + j, NY)]
+            start(src, wide_in.at[q, n], s_wide.at[q, n], r_wide.at[q, n], near[(dxh, j)])
+
+    def collect(q):
+        value = decode(wide_out[q, xh * NY + y], 16)
+        for n, key in enumerate(YX):
+            send_to(wide_in.at[q, n], wide_in.at[q, n], s_wide.at[q, n], r_wide.at[q, n], near[key]).wait_recv()
+            value = value + decode(wide_in[q, n], 16)
+        for i in range(4):
+            k = ORDER[4 * q + i]
+            part = value[OWN * i : OWN * i + OWN]
+            if k == 0:
+                rest_own[...] = part
+            else:
+                line_out[k - 1] = encode(part, 8)
+                start(line_out.at[k - 1], line_in.at[k - 1], s_line.at[k - 1], r_line.at[k - 1], z_peers[k - 1])
+
     compute(0)
     compute(1)
+    chunk(0)
     ring_up(0, 0)
-    ring_down(0, None)
+    ring_down(0, 0)
     compute(2)
     compute(3)
     for n, key in enumerate(GROUP):
@@ -411,8 +503,12 @@
     loss_y[0] = jnp.sum(loss_group[...], axis=0)
     for j in range(1, NY):
         start(loss_y.at[0], loss_y.at[j], s_ly.at[j - 1], r_ly.at[j - 1], y_peers[j - 1])
+    chunk(1)
     ring_up(1, 1)
+    chunk(2)
     ring_down(1, 2)
+    chunk(3)
+    spread(0)
     compute(4)
     compute(5)
     for j in range(1, NY):
@@ -420,43 +516,57 @@
     loss_z[0] = jnp.sum(loss_y[...], axis=0)
     for k in range(1, NZ):
         start(loss_z.at[0], loss_z.at[k], s_lz.at[k - 1], r_lz.at[k - 1], z_peers[k - 1])
+    chunk(4)
     ring_up(2, 3)
     ring_down(2, 4)
     compute(6)
     compute(7)
+    for n in (5, 6, 7):
+        chunk(n)
+    spread(1)
     ring_up(3, 5)
     ring_down(3, 6)
+    collect(0)
+    collect(1)
     for k in range(1, NZ):
         send_to(loss_z.at[0], loss_z.at[k], s_lz.at[k - 1], r_lz.at[k - 1], z_peers[k - 1]).wait_recv()
     loss_out_ref[...] = jnp.sum(loss_z[...], axis=0)
-    t = chunk(7)
-    own = []
+    for copy in copies:
+        copy.wait_send()
+    del copies[:]
+    t = lax.rem(z + ORDER[7], NZ)
     for h in range(SUBS):
         at = slice(h * SUB, h * SUB + SUB)
         value = terms[c, t, :, at] + sibling[t, :, at]
         send_to(up_out.at[3, h], up_in.at[3, h], s_rup.at[3, h], r_rup.at[3, h], up).wait_recv()
         value = value + decode(up_in[3, h], 16)
         send_to(down_out.at[3, h], down_in.at[3, h], s_rdown.at[3, h], r_rdown.at[3, h], down).wait_recv()
-        own.append(value + decode(down_in[3, h], 16))
-    own = jnp.concatenate(own, axis=1).reshape(2 * NY, OWN, H)
-    for i in range(2 * NY):
-        near_out[i] = encode(own[i], 8)
+        value = (value + decode(down_in[3, h], 16)).reshape(2 * NY, OWN, SUB)
+        for i in range(2 * NY):
+            near_out[i, :, at] = encode(value[i], 8)
     for n, (dxh, j) in enumerate(YX):
         src = near_out.at[lax.rem(xh + dxh, 2) * NY + lax.rem(y + j, NY)]
         start(src, near_in.at[n], s_near.at[n], r_near.at[n], near[(dxh, j)])
+    rest = rest_own[...]
+    for k in range(1, NZ):
+        send_to(line_in.at[k - 1], line_in.at[k - 1], s_line.at[k - 1], r_line.at[k - 1], z_peers[k - 1]).wait_recv()
+        rest = rest + decode(line_in[k - 1], 8)
+    final[c, :, FAR:] = rest
     result = decode(near_out[xh * NY + y], 8)
     for n, key in enumerate(YX):
         send_to(near_in.at[n], near_in.at[n], s_near.at[n], r_near.at[n], near[key]).wait_recv()
         result = result + decode(near_in[n], 8)
-    final[c] = result
+    final[c, :, :FAR] = result
     start(final.at[c], final.at[c], s_final, r_final, twin)
     send_to(final.at[1 - c], final.at[1 - c], s_final, r_final, twin).wait_recv()
-    out_ref[...] = final[...]
+    even = c == 0
+    image_out_ref[...] = jnp.where(even, final[0, 0:12, :], final[0, 12:24, :])
+    text_out_ref[...] = jnp.where(even, final[1, 0:12, :], final[1, 12:24, :])
     for copy in copies:
         copy.wait_send()
 
 
-def run_kernel(pooled, count, logit_scale, logit_bias, loss_scale, image, text, image_pre, text_pre):
+def run_kernel(count, logit_scale, logit_bias, loss_scale, image, text, image_weight, text_weight):
     dma = pltpu.SemaphoreType.DMA
     vmem = pl.BlockSpec(memory_space=pltpu.VMEM)
     smem = pl.BlockSpec(memory_space=pltpu.SMEM)
@@ -466,12 +576,19 @@
     tile = (8, 128)
     return pl.pallas_call(
         kernel,
-        out_shape=(jax.ShapeDtypeStruct((2, OWN, H), F32), jax.ShapeDtypeStruct(tile, F32)),
-        in_specs=[vmem, vmem, smem, smem, smem, anywhere, anywhere, anywhere, anywhere],
-        out_specs=(vmem, vmem),
+        out_shape=(
+            jax.ShapeDtypeStruct((12, H), F32),
+            jax.ShapeDtypeStruct((12, H), F32),
+            jax.ShapeDtypeStruct(tile, F32),
+        ),
+        in_specs=[vmem, smem, smem, smem, anywhere, anywhere, anywhere, anywhere],
+        out_specs=(vmem, vmem, vmem),
         scratch_shapes=[
-            pltpu.VMEM((16, H + EXT), F32),
-            pltpu.VMEM((16, H + EXT), F32),
+            pltpu.VMEM((D, H), BF16),
+            pltpu.VMEM((D, H), BF16),
+            pltpu.VMEM((32, H), F32),
+            pltpu.VMEM((2, 8, H + EXT), F32),
+            pltpu.VMEM((2, 8, H + EXT), F32),
             pltpu.VMEM((4,) + tile, F32),
             pltpu.VMEM((NZ, NY, 16, D + EXT), BF16),
             pltpu.VMEM((8, 16, D + EXT), BF16),
@@ -492,15 +609,20 @@
             ring,
             ring,
             ring,
-            pltpu.VMEM((2 * NY, 32, H), jnp.int16),
-            pltpu.VMEM((7, 32, H), jnp.int16),
+            pltpu.VMEM((2 * NY, 32, FAR), jnp.int16),
+            pltpu.VMEM((7, 32, FAR), jnp.int16),
+            pltpu.VMEM((2, 2 * NY, 112, REST), jnp.int16),
+            pltpu.VMEM((2, 7, 112, REST), jnp.int16),
+            pltpu.VMEM((7, 32, REST), jnp.int16),
+            pltpu.VMEM((7, 32, REST), jnp.int16),
+            pltpu.VMEM((OWN, REST), F32),
             pltpu.VMEM((2, OWN, H), F32),
             pltpu.VMEM((8,) + tile, F32),
             pltpu.VMEM((NY,) + tile, F32),
             pltpu.VMEM((NZ,) + tile, F32),
-            dma((4,)),
+            dma((8,)),
         ]
-        + [dma] * 2
+        + [dma((2,))] * 2
         + [dma((3,))] * 2
         + [dma((7,))] * 2
         + [dma((3,))] * 2
@@ -509,6 +631,8 @@
         + [dma((8,))] * 2
         + [dma((4, SUBS))] * 4
         + [dma((7,))] * 2
+        + [dma((2, 7))] * 2
+        + [dma((7,))] * 2
         + [dma] * 2
         + [dma((7,))] * 2
         + [dma((3,))] * 2
@@ -516,16 +640,7 @@
         compiler_params=pltpu.CompilerParams(
             collective_id=1, has_side_effects=True, vmem_limit_bytes=58 * 1024 * 1024
         ),
-    )(pooled, count, logit_scale, logit_bias, loss_scale, image, text, image_pre, text_pre)
-
-
-def tower_block(tokens, weight, offset):
-    flat_tokens = tokens.reshape(-1, tokens.shape[2])
-    preact = jnp.dot(flat_tokens, weight, preferred_element_type=F32)
-    residual = lax.dynamic_slice_in_dim(flat_tokens, offset, weight.shape[1], 1).astype(F32)
-    hidden = residual + jax.nn.gelu(preact, approximate=True)
-    pooled = jnp.mean(hidden.reshape(tokens.shape[0], tokens.shape[1], -1), axis=1)
-    return (flat_tokens, preact, pooled)
+    )(count, logit_scale, logit_bias, loss_scale, image, text, image_weight, text_weight)
 
 
 def body(
@@ -538,17 +653,18 @@
     loss_scale,
     valid_count,
 ):
-    core = lax.rem(lax.axis_index("dp"), 2)
-    half_start = lax.axis_index("mp") * H
-    image_flat, image_preact, image_pooled = tower_block(image_tokens, image_weight, half_start)
-    text_flat, text_preact, text_pooled = tower_block(text_tokens, text_weight, half_start)
-    pooled = jnp.concatenate([image_pooled[:8], text_pooled[:8], image_pooled[8:], text_pooled[8:]], axis=0)
     count = jnp.broadcast_to(valid_count.astype(F32)[:, None], (8, 128))
-    grads_out, loss = run_kernel(
-        pooled, count, logit_scale, logit_bias, loss_scale, image_flat, text_flat, image_preact, text_preact
+    image_grad, text_grad, loss = run_kernel(
+        count,
+        logit_scale,
+        logit_bias,
+        loss_scale,
+        image_tokens.reshape(-1, D),
+        text_tokens.reshape(-1, D),
+        image_weight,
+        text_weight,
     )
-    mine = lax.dynamic_slice_in_dim(grads_out, core * 12, 12, 1)
-    return (loss[0, 0], mine[0], mine[1])
+    return (loss[0, 0], image_grad, text_grad)
 
 
 def solution(mesh):

time: 108 us -> 95 us (0.88)
  matrix products: 10.2 us -> 0 us
  Pallas kernels: 88.6 us -> 86.8 us
    dot_general x2 -> x0, matrix products: 10.2 us -> none  [tower_block(): preact = jnp.dot(flat_tokens, weight, preferred_element_type=F32)]
    pallas_call x1, Pallas kernels: 88.6 us -> 86.8 us  [run_kernel(): pl.pallas_call(kernel, out_shape=(jax.ShapeDtypeStruct((12, H), F32), jax...]
    squeeze x1 -> x0, local copies, waits for them, and re-layouts: 1.48 us -> none  [body(): return (loss[0, 0], mine[0], mine[1])]
    unnamed x6 -> x2, local copies, waits for them, and re-layouts: 1.66 us -> 2.84 us
where the time goes in v3:
time: 95 us; the launch traced here: 94.7 us
  Pallas kernels  86.8 us (91%)
  local copies, waits for them, and re-layouts  4.63 us (5%)
  between operations  3.22 us (3%)
    pallas_call x1, Pallas kernels, run_kernel(): pl.pallas_call(kernel, out_shape=(jax.ShapeDtypeStruct((12, H), F32), jax...  86.8 us
    unnamed x2, local copies, waits for them, and re-layouts  2.84 us

profile of v3, /device:TPU:1, one launch (start us, length us, event | category | flops | bytes accessed | tf_op | source)
XLA Modules:
  0.0 94.7 jit_solution(4438570809918084536)
XLA Ops:
  3.2 0.6 broadcast_in_dim.9.count_ref
  3.8 86.8 %shard_map.103 = (f32[12,768]{1,0:T(8,128)}, f32[12,768]{1,0:T(8,128)}, f32[8,128]{1,0:T(8,128)}) custom-call(f32[8,128]{1,0:T(8,128)} %broadcast_in_dim.9.count_ref, f32[1]{0:T(128)S(6)} %copy.13.scale_ref, f32[1]{0:T(128)S(6)} %copy.14.bias_ref, f32[1]{0:T(128)S(6)} %copy.15.loss_scale_ref, bf16[1024,1536]{1,0:T(8,128)(2,1)} %bitcast.4, ...), custom_call_target="tpu_custom_call" | custom-call | tf_op jit(solution)/shard_map/pallas_call | solution.py:577
  90.6 1.2 %slice.3 = f32[1,1]{1,0:T(1,128)} slice(f32[8,128]{1,0:T(8,128)} %get-tuple-element.6), slice={[0:1], [0:1]} | slice | bytes 8 | tf_op jit(solution)/shard_map/slice | solution.py:667
  91.8 1.4 %copy.17 = f32[12,768]{1,0:T(8,128)} copy(f32[12,768]{1,0:T(8,128)} %get-tuple-element.13) | data formatting | bytes 73728
  93.2 1.4 %copy.18 = f32[12,768]{1,0:T(8,128)} copy(f32[12,768]{1,0:T(8,128)} %get-tuple-element.14) | data formatting | bytes 73728

commit v4 on v3

--- a/solution.py
+++ b/solution.py
@@ -100,8 +100,9 @@
 YX = [(dxh, j) for dxh in range(2) for j in range(NY) if (dxh, j) != (0, 0)]
 PAIRS = [(0, 1), (2, 0), (2, 1)]
 ORDER = [4, 3, 5, 2, 6, 1, 7, 0]
-SUBS = 2
-SUB = 256
+SUBS = 3
+UPS = 2
+SUB = 128
 FAR = SUBS * SUB
 REST = H - FAR
 
@@ -125,6 +126,7 @@
     half_in,
     counts,
     plane,
+    upper,
     group,
     parts,
     landed,
@@ -138,7 +140,8 @@
     image_gpre,
     text_gpre,
     terms,
-    sibling,
+    sib_out,
+    sib_in,
     up_out,
     up_in,
     down_out,
@@ -167,6 +170,10 @@
     r_up,
     s_down,
     r_down,
+    s_uz,
+    r_uz,
+    s_uy,
+    r_uy,
     s_part,
     r_part,
     s_sib,
@@ -265,7 +272,8 @@
     pool(text_tok, text_pre, 1, 32, 8)
     pl.semaphore_wait(barrier, len(peers))
     swap(1)
-    counts[pair_slot] = count_ref[...]
+    own_count = jnp.full((8, 128), count_ref[0], jnp.int32).astype(F32)
+    counts[pair_slot] = own_count
     for n, key in enumerate(PAIRS):
         start(counts.at[pair_slot], counts.at[pair_slot], s_count.at[n], r_count.at[n], members[key])
     for p in range(1, 4):
@@ -297,13 +305,14 @@
         slot = lax.rem(xh + dx // 2, 2) * 2 + lax.rem(c + dc, NC)
         send_to(counts.at[slot], counts.at[slot], s_count.at[n], r_count.at[n], members[(dx, dc)]).wait_recv()
     row_total = jnp.sum(counts[...], axis=0)[0:1, :]
-    own_count = count_ref[0:1, :]
+    own_count = own_count[0:1, :]
     sample = lax.rem(lax.broadcasted_iota(jnp.int32, (16, EXT), 0), 8) + 8 * lo
     lane = lax.broadcasted_iota(jnp.int32, (16, EXT), 1)
     usable = jnp.where(sample.astype(F32) < own_count, 1.0, 0.0)
     extra = jnp.where(lane < EXT // 2, usable, jnp.broadcast_to(row_total, (16, EXT)))
     block = jnp.concatenate([low.astype(BF16), high.astype(BF16), extra.astype(BF16)], axis=1)
-    plane[z, y] = block
+    plane[z, y] = block[:, :H]
+    upper[z, y] = block[:, H:]
     group[me] = block
 
     def pass_up(step, j, zs, ys):
@@ -311,11 +320,24 @@
 
     def pass_down(step, j, zs, ys):
         start(plane.at[zs, ys], plane.at[zs, ys], s_down.at[step, j], r_down.at[step, j], down)
+
+    def pass_y(k):
+        zs = lax.rem(z + k, NZ)
+        for j in range(1, NY):
+            start(upper.at[zs, y], upper.at[zs, y], s_uy.at[k, j - 1], r_uy.at[k, j - 1], y_peers[j - 1])
+
+    def land_z(k):
+        zs = lax.rem(z + k, NZ)
+        send_to(upper.at[zs, y], upper.at[zs, y], s_uz.at[NZ - k - 1], r_uz.at[NZ - k - 1], up).wait_recv()
+        pass_y(k)
 
     for j in range(1, NY):
         start(plane.at[z, y], plane.at[z, y], s_y.at[j - 1], r_y.at[j - 1], y_peers[j - 1])
     pass_up(0, 0, z, y)
     pass_down(0, 0, z, y)
+    for k in (1, 7, 2, 6, 3, 5, 4):
+        start(upper.at[z, y], upper.at[z, y], s_uz.at[k - 1], r_uz.at[k - 1], z_peers[k - 1])
+    pass_y(0)
     for n, key in enumerate(GROUP):
         start(group.at[me], group.at[me], s_group.at[n], r_group.at[n], members[key])
 
@@ -363,20 +385,37 @@
                 send_to(plane.at[zs, ys], plane.at[zs, ys], s_down.at[step, j], r_down.at[step, j], down).wait_recv()
                 if step < 2 or (step == 2 and j >= 2):
                     pass_down(step + 1, j, zs, ys)
+            if step == 0 and j == 0:
+                land_z(1)
+                land_z(7)
+            if step == 0 and j == 2:
+                land_z(2)
+                land_z(6)
+            if step == 1 and j == 0:
+                land_z(3)
+                land_z(5)
+                land_z(4)
             idle(2 if step < 1 else 1)
     idle(len(pieces) - done[0])
     for n, key in enumerate(GROUP):
         slot = slot_of(*sources[key])
         send_to(group.at[slot], group.at[slot], s_group.at[n], r_group.at[n], members[key]).wait_recv()
 
+    for k in range(NZ):
+        for j in range(1, NY):
+            zs, ys = lax.rem(z + k, NZ), lax.rem(y + NY - j, NY)
+            send_to(upper.at[zs, ys], upper.at[zs, ys], s_uy.at[k, j - 1], r_uy.at[k, j - 1], up).wait_recv()
+
     rows = group[...].reshape(8 * 16, D + EXT)
-    cols = plane[...].reshape(32 * 16, D + EXT)
-    row_main, col_main = rows[:, :D], cols[:, :D]
+    low_cols = plane[...].reshape(32 * 16, H)
+    high_cols = upper[...].reshape(32 * 16, H + EXT)
+    row_main, high_main = rows[:, :D], high_cols[:, :H]
     logit_mult = scale_ref[0]
-    logits = logit_mult * dot_t(row_main, col_main) + bias_ref[0]
+    products = dot_t(row_main[:, :H], low_cols) + dot_t(row_main[:, H:], high_main)
+    logits = logit_mult * products + bias_ref[0]
     pick = lax.broadcasted_iota(jnp.int32, (16, EXT), 0) * (EXT // 2)
     pick = jnp.where(pick == lax.broadcasted_iota(jnp.int32, (16, EXT), 1), 1.0, 0.0).astype(BF16)
-    col_extra = dot_t(pick, cols[:, D:])
+    col_extra = dot_t(pick, high_cols[:, H:])
     total = jnp.sum(col_extra[1:2, :]) * (1.0 / 16.0)
     col_usable = col_extra[0:1, :]
     row_usable = rows[:, D : D + 1].astype(F32)
@@ -391,7 +430,9 @@
     margin = -sign * logits
     coeff = loss_scale_ref[0] / total
     dlogit = (jnp.where(used, -sign * jax.nn.sigmoid(margin), 0.0) * coeff).astype(BF16)
-    grad = logit_mult * jnp.dot(dlogit, col_main, preferred_element_type=F32)
+    grad = logit_mult * jnp.concatenate(
+        [jnp.dot(dlogit, cols, preferred_element_type=F32) for cols in (low_cols, high_main)], axis=1
+    )
     radial = jnp.sum(row_main.astype(F32) * grad, axis=1, keepdims=True)
     code = code_of(jnp.max(jnp.abs(grad), axis=1, keepdims=True))
     factor = jnp.exp2(TOP - code / CODE)
@@ -438,39 +479,38 @@
 
     def compute(n):
         t = lax.rem(z + ORDER[n], NZ)
-        terms[0, t] = jnp.dot(image_t[t], image_gpre[...], preferred_element_type=F32)
-        terms[1, t] = jnp.dot(text_t[t], text_gpre[...], preferred_element_type=F32)
-        start(terms.at[1 - c, t], sibling.at[t], s_sib.at[n], r_sib.at[n], twin)
+        image = jnp.dot(image_t[t], image_gpre[...], preferred_element_type=F32)
+        text = jnp.dot(text_t[t], text_gpre[...], preferred_element_type=F32)
+        terms[n] = jnp.where(c == 0, image, text)
+        sib_out[n] = encode(jnp.where(c == 0, text, image), 16)
+        start(sib_out.at[n], sib_in.at[n], s_sib.at[n], r_sib.at[n], twin)
 
     def chunk(n):
-        t = lax.rem(z + ORDER[n], NZ)
-        send_to(sibling.at[t], sibling.at[t], s_sib.at[n], r_sib.at[n], twin).wait_recv()
-        return t
-
-    def ring(step, n, out, inn, send_sem, recv_sem, way, split):
-        t = lax.rem(z + ORDER[n], NZ)
-        for h in range(SUBS):
-            if step == 0 and h != split:
-                continue
-            at = slice(h * SUB, h * SUB + SUB)
-            value = terms[c, t, :, at] + sibling[t, :, at]
-            if step > 1 or (step == 1 and h == split):
-                send_to(out.at[step - 1, h], inn.at[step - 1, h], send_sem.at[step - 1, h], recv_sem.at[step - 1, h], way).wait_recv()
-                value = value + decode(inn[step - 1, h], 16)
-            out[step, h] = encode(value, 16)
-            start(out.at[step, h], inn.at[step, h], send_sem.at[step, h], recv_sem.at[step, h], way)
-
-    def ring_up(step, n):
-        ring(step, n, up_out, up_in, s_rup, r_rup, up, 0)
-
-    def ring_down(step, n):
-        ring(step, n, down_out, down_in, s_rdown, r_rdown, down, 1)
+        send_to(sib_out.at[n], sib_in.at[n], s_sib.at[n], r_sib.at[n], twin).wait_recv()
+        terms[n] += decode(sib_in[n], 16)
+
+    def ring(step, n, h, out, inn, send_sem, recv_sem, way, early):
+        value = terms[n, :, h * SUB : h * SUB + SUB]
+        if step > 1 or (step == 1 and early):
+            send_to(out.at[step - 1, h], inn.at[step - 1, h], send_sem.at[step - 1, h], recv_sem.at[step - 1, h], way).wait_recv()
+            value = value + decode(inn[step - 1, h], 16)
+        out[step, h] = encode(value, 16)
+        start(out.at[step, h], inn.at[step, h], send_sem.at[step, h], recv_sem.at[step, h], way)
+
+    def ring_step(step, n_up, n_down):
+        ups, downs = list(range(UPS)), list(range(UPS, SUBS))
+        if step > 0:
+            ups, downs = downs + ups, ups + downs
+        for i in range(SUBS):
+            if i < len(ups):
+                ring(step, n_up, ups[i], up_out, up_in, s_rup, r_rup, up, ups[i] < UPS)
+            if i < len(downs):
+                ring(step, n_down, downs[i], down_out, down_in, s_rdown, r_rdown, down, downs[i] >= UPS)
 
     def spread(q):
         values = []
         for n in range(4 * q, 4 * q + 4):
-            t = lax.rem(z + ORDER[n], NZ)
-            values.append((terms[c, t, :, FAR:] + sibling[t, :, FAR:]).reshape(2 * NY, OWN, REST))
+            values.append(terms[n, :, FAR:].reshape(2 * NY, OWN, REST))
         for i in range(2 * NY):
             wide_out[q, i] = encode(jnp.concatenate([value[i] for value in values], axis=0), 16)
         for n, (dxh, j) in enumerate(YX):
@@ -494,50 +534,40 @@
     compute(0)
     compute(1)
     chunk(0)
-    ring_up(0, 0)
-    ring_down(0, 0)
+    ring_step(0, 0, 0)
     compute(2)
     compute(3)
+    for n in (1, 2, 3):
+        chunk(n)
+    spread(0)
+    compute(4)
+    compute(5)
+    ring_step(1, 1, 2)
+    compute(6)
+    compute(7)
+    for n in (4, 5, 6, 7):
+        chunk(n)
+    spread(1)
     for n, key in enumerate(GROUP):
         send_to(loss_group.at[0], loss_group.at[n + 1], s_lg.at[n], r_lg.at[n], members[key]).wait_recv()
     loss_y[0] = jnp.sum(loss_group[...], axis=0)
     for j in range(1, NY):
         start(loss_y.at[0], loss_y.at[j], s_ly.at[j - 1], r_ly.at[j - 1], y_peers[j - 1])
-    chunk(1)
-    ring_up(1, 1)
-    chunk(2)
-    ring_down(1, 2)
-    chunk(3)
-    spread(0)
-    compute(4)
-    compute(5)
+    ring_step(2, 3, 4)
+    collect(0)
     for j in range(1, NY):
         send_to(loss_y.at[0], loss_y.at[j], s_ly.at[j - 1], r_ly.at[j - 1], y_peers[j - 1]).wait_recv()
     loss_z[0] = jnp.sum(loss_y[...], axis=0)
     for k in range(1, NZ):
         start(loss_z.at[0], loss_z.at[k], s_lz.at[k - 1], r_lz.at[k - 1], z_peers[k - 1])
-    chunk(4)
-    ring_up(2, 3)
-    ring_down(2, 4)
-    compute(6)
-    compute(7)
-    for n in (5, 6, 7):
-        chunk(n)
-    spread(1)
-    ring_up(3, 5)
-    ring_down(3, 6)
-    collect(0)
+    ring_step(3, 5, 6)
     collect(1)
-    for k in range(1, NZ):
-        send_to(loss_z.at[0], loss_z.at[k], s_lz.at[k - 1], r_lz.at[k - 1], z_peers[k - 1]).wait_recv()
-    loss_out_ref[...] = jnp.sum(loss_z[...], axis=0)
     for copy in copies:
         copy.wait_send()
     del copies[:]
-    t = lax.rem(z + ORDER[7], NZ)
     for h in range(SUBS):
         at = slice(h * SUB, h * SUB + SUB)
-        value = terms[c, t, :, at] + sibling[t, :, at]
+        value = terms[7, :, at]
         send_to(up_out.at[3, h], up_in.at[3, h], s_rup.at[3, h], r_rup.at[3, h], up).wait_recv()
         value = value + decode(up_in[3, h], 16)
         send_to(down_out.at[3, h], down_in.at[3, h], s_rdown.at[3, h], r_rdown.at[3, h], down).wait_recv()
@@ -556,6 +586,9 @@
     for n, key in enumerate(YX):
         send_to(near_in.at[n], near_in.at[n], s_near.at[n], r_near.at[n], near[key]).wait_recv()
         result = result + decode(near_in[n], 8)
+    for k in range(1, NZ):
+        send_to(loss_z.at[0], loss_z.at[k], s_lz.at[k - 1], r_lz.at[k - 1], z_peers[k - 1]).wait_recv()
+    loss_out_ref[...] = jnp.sum(loss_z[...], axis=0)
     final[c, :, :FAR] = result
     start(final.at[c], final.at[c], s_final, r_final, twin)
     send_to(final.at[1 - c], final.at[1 - c], s_final, r_final, twin).wait_recv()
@@ -570,7 +603,7 @@
     dma = pltpu.SemaphoreType.DMA
     vmem = pl.BlockSpec(memory_space=pltpu.VMEM)
     smem = pl.BlockSpec(memory_space=pltpu.SMEM)
-    anywhere = pl.BlockSpec(memory_space=pl.ANY)
+    anywhere = pl.BlockSpec(memory_space=pltpu.HBM)
     image_rows, text_rows = image.shape[0], text.shape[0]
     ring = pltpu.VMEM((4, SUBS, ZROWS + 16, SUB), jnp.int16)
     tile = (8, 128)
@@ -581,7 +614,7 @@
             jax.ShapeDtypeStruct((12, H), F32),
             jax.ShapeDtypeStruct(tile, F32),
         ),
-        in_specs=[vmem, smem, smem, smem, anywhere, anywhere, anywhere, anywhere],
+        in_specs=[smem, smem, smem, smem, anywhere, anywhere, anywhere, anywhere],
         out_specs=(vmem, vmem, vmem),
         scratch_shapes=[
             pltpu.VMEM((D, H), BF16),
@@ -590,7 +623,8 @@
             pltpu.VMEM((2, 8, H + EXT), F32),
             pltpu.VMEM((2, 8, H + EXT), F32),
             pltpu.VMEM((4,) + tile, F32),
-            pltpu.VMEM((NZ, NY, 16, D + EXT), BF16),
+            pltpu.VMEM((NZ, NY, 16, H), BF16),
+            pltpu.VMEM((NZ, NY, 16, H + EXT), BF16),
             pltpu.VMEM((8, 16, D + EXT), BF16),
             pltpu.VMEM((4, 2, 32, H + EXT), jnp.int16),
             pltpu.VMEM((8, 32, H + EXT), jnp.int16),
@@ -603,8 +637,9 @@
             pltpu.VMEM((text_rows, H), F32),
             pltpu.VMEM((image_rows, H), BF16),
             pltpu.VMEM((text_rows, H), BF16),
-            pltpu.VMEM((2, NZ, ZROWS, H), F32),
             pltpu.VMEM((NZ, ZROWS, H), F32),
+            pltpu.VMEM((NZ, ZROWS + 16, H), jnp.int16),
+            pltpu.VMEM((NZ, ZROWS + 16, H), jnp.int16),
             ring,
             ring,
             ring,
@@ -628,6 +663,8 @@
         + [dma((3,))] * 2
         + [dma((4, 4))] * 4
         + [dma((7,))] * 2
+        + [dma((NZ, 3))] * 2
+        + [dma((7,))] * 2
         + [dma((8,))] * 2
         + [dma((4, SUBS))] * 4
         + [dma((7,))] * 2
@@ -638,7 +675,7 @@
         + [dma((3,))] * 2
         + [dma((7,))] * 2,
         compiler_params=pltpu.CompilerParams(
-            collective_id=1, has_side_effects=True, vmem_limit_bytes=58 * 1024 * 1024
+            collective_id=1, has_side_effects=True, vmem_limit_bytes=53 * 1024 * 1024
         ),
     )(count, logit_scale, logit_bias, loss_scale, image, text, image_weight, text_weight)
 
@@ -653,9 +690,8 @@
     loss_scale,
     valid_count,
 ):
-    count = jnp.broadcast_to(valid_count.astype(F32)[:, None], (8, 128))
     image_grad, text_grad, loss = run_kernel(
-        count,
+        valid_count,
         logit_scale,
         logit_bias,
         loss_scale,

time: 95 us -> 89.1 us (0.938)
  local copies, waits for them, and re-layouts: 4.63 us -> 1.75 us
  Pallas kernels: 86.8 us -> 84 us
    pallas_call x1, Pallas kernels: 86.8 us -> 84 us  [run_kernel(): pl.pallas_call(kernel, out_shape=(jax.ShapeDtypeStruct((12, H), F32), jax...]
    unnamed x2, local copies, waits for them, and re-layouts: 2.84 us -> 1.24 us
where the time goes in v4:
time: 89.1 us; the launch traced here: 88.9 us
  Pallas kernels  84 us (94%)
  between operations  3.22 us (4%)
  local copies, waits for them, and re-layouts  1.75 us (2%)
    pallas_call x1, Pallas kernels, run_kernel(): pl.pallas_call(kernel, out_shape=(jax.ShapeDtypeStruct((12, H), F32), jax...  84 us

profile of v4, /device:TPU:1, one launch (start us, length us, event | category | flops | bytes accessed | tf_op | source)
XLA Modules:
  0.0 88.9 jit_solution(13436407996387070980)
XLA Ops:
  3.2 84.0 %shard_map.103 = (f32[12,768]{1,0:T(8,128)S(1)}, f32[12,768]{1,0:T(8,128)S(1)}, f32[8,128]{1,0:T(8,128)S(1)}) custom-call(s32[1]{0:T(128)S(6)} %copy.16.count_ref, f32[1]{0:T(128)S(6)} %copy.13.scale_ref, f32[1]{0:T(128)S(6)} %copy.14.bias_ref, f32[1]{0:T(128)S(6)} %copy.15.loss_scale_ref, bf16[1024,1536]{1,0:T(8,128)(2,1)} %bitcast.3, ...), custom_call_target="tpu_custom_call" | custom-call | tf_op jit(solution)/shard_map/pallas_call | solution.py:610
  87.2 0.5 slice.3
  87.7 0.6 copy.17
  88.3 0.6 copy.18

commit v5 on v4

--- a/solution.py
+++ b/solution.py
@@ -99,8 +99,10 @@
 
 YX = [(dxh, j) for dxh in range(2) for j in range(NY) if (dxh, j) != (0, 0)]
 PAIRS = [(0, 1), (2, 0), (2, 1)]
+LOW = 640
+LINE = [0, 1, 3, 2]
 ORDER = [4, 3, 5, 2, 6, 1, 7, 0]
-SUBS = 3
+SUBS = 4
 UPS = 2
 SUB = 128
 FAR = SUBS * SUB
@@ -108,10 +110,10 @@
 
 
 def kernel(
-    count_ref,
-    scale_ref,
-    bias_ref,
-    loss_scale_ref,
+    count_hbm,
+    scale_hbm,
+    bias_hbm,
+    loss_scale_hbm,
     image_ref,
     text_ref,
     image_weight_ref,
@@ -119,6 +121,10 @@
     image_out_ref,
     text_out_ref,
     loss_out_ref,
+    count_ref,
+    scale_ref,
+    bias_ref,
+    loss_scale_ref,
     image_weight,
     text_weight,
     pooled,
@@ -222,6 +228,10 @@
         loads[name] = pltpu.make_async_copy(src, dst, s_load.at[len(loads)])
         loads[name].start()
 
+    fetch("count", count_hbm, count_ref)
+    fetch("scale", scale_hbm, scale_ref)
+    fetch("bias", bias_hbm, bias_ref)
+    fetch("loss", loss_scale_hbm, loss_scale_ref)
     fetch("tw", text_weight_ref, text_weight)
     for p in range(2):
         at = pl.ds(256 * p, 256)
@@ -272,6 +282,8 @@
     pool(text_tok, text_pre, 1, 32, 8)
     pl.semaphore_wait(barrier, len(peers))
     swap(1)
+    for name in ("count", "scale", "bias", "loss"):
+        loads[name].wait()
     own_count = jnp.full((8, 128), count_ref[0], jnp.int32).astype(F32)
     counts[pair_slot] = own_count
     for n, key in enumerate(PAIRS):
@@ -311,32 +323,61 @@
     usable = jnp.where(sample.astype(F32) < own_count, 1.0, 0.0)
     extra = jnp.where(lane < EXT // 2, usable, jnp.broadcast_to(row_total, (16, EXT)))
     block = jnp.concatenate([low.astype(BF16), high.astype(BF16), extra.astype(BF16)], axis=1)
-    plane[z, y] = block[:, :H]
-    upper[z, y] = block[:, H:]
+    plane[z, y] = block[:, :LOW]
+    upper[z, y] = block[:, LOW:]
     group[me] = block
 
-    def pass_up(step, j, zs, ys):
-        start(plane.at[zs, ys], plane.at[zs, ys], s_up.at[step, j], r_up.at[step, j], up)
-
-    def pass_down(step, j, zs, ys):
-        start(plane.at[zs, ys], plane.at[zs, ys], s_down.at[step, j], r_down.at[step, j], down)
+    def pass_up(far, j, zs, ys, hops):
+        start(plane.at[zs, ys], plane.at[zs, ys], s_up.at[far, j], r_up.at[far, j], z_peers[hops - 1])
+
+    def pass_down(far, j, zs, ys, hops):
+        start(plane.at[zs, ys], plane.at[zs, ys], s_down.at[far, j], r_down.at[far, j], z_peers[NZ - hops - 1])
+
+    def send_line(j, ys):
+        for hops in (2, 1):
+            pass_up(hops - 1, j, z, ys, hops)
+            pass_down(hops - 1, j, z, ys, hops)
+
+    def land_up(far, j):
+        zs, ys = lax.rem(z + NZ - far - 1, NZ), lax.rem(y + NY - j, NY)
+        send_to(plane.at[zs, ys], plane.at[zs, ys], s_up.at[far, j], r_up.at[far, j], up).wait_recv()
+        if far == 1:
+            if j < 2:
+                pass_up(3, j, zs, ys, 2)
+            pass_up(2, j, zs, ys, 1)
+
+    def land_down(far, j):
+        zs, ys = lax.rem(z + far + 1, NZ), lax.rem(y + NY - j, NY)
+        send_to(plane.at[zs, ys], plane.at[zs, ys], s_down.at[far, j], r_down.at[far, j], down).wait_recv()
+        if far == 1:
+            if j >= 2:
+                pass_down(3, j, zs, ys, 2)
+            pass_down(2, j, zs, ys, 1)
 
     def pass_y(k):
         zs = lax.rem(z + k, NZ)
         for j in range(1, NY):
             start(upper.at[zs, y], upper.at[zs, y], s_uy.at[k, j - 1], r_uy.at[k, j - 1], y_peers[j - 1])
 
+    def send_z(k, n, way):
+        zs = lax.rem(z + k, NZ)
+        start(upper.at[zs, y], upper.at[zs, y], s_uz.at[n], r_uz.at[n], way)
+
     def land_z(k):
         zs = lax.rem(z + k, NZ)
         send_to(upper.at[zs, y], upper.at[zs, y], s_uz.at[NZ - k - 1], r_uz.at[NZ - k - 1], up).wait_recv()
+        if k < 3:
+            send_z(k, NZ - k - 2, down)
+        if k > 5:
+            send_z(k, NZ - k, up)
         pass_y(k)
 
     for j in range(1, NY):
         start(plane.at[z, y], plane.at[z, y], s_y.at[j - 1], r_y.at[j - 1], y_peers[j - 1])
-    pass_up(0, 0, z, y)
-    pass_down(0, 0, z, y)
-    for k in (1, 7, 2, 6, 3, 5, 4):
-        start(upper.at[z, y], upper.at[z, y], s_uz.at[k - 1], r_uz.at[k - 1], z_peers[k - 1])
+    send_line(0, y)
+    send_z(0, 0, up)
+    send_z(0, 6, down)
+    send_z(0, 3, z_peers[3])
     pass_y(0)
     for n, key in enumerate(GROUP):
         start(group.at[me], group.at[me], s_group.at[n], r_group.at[n], members[key])
@@ -366,36 +407,33 @@
             piece()
         done[0] += amount
 
-    for j in range(1, NY):
+    for j in LINE[1:]:
         ys = lax.rem(y + NY - j, NY)
         send_to(plane.at[z, ys], plane.at[z, ys], s_y.at[j - 1], r_y.at[j - 1], up).wait_recv()
-        pass_up(0, j, z, ys)
-        pass_down(0, j, z, ys)
+        send_line(j, ys)
+    land_z(1)
+    land_z(7)
     idle()
-    for step in range(4):
-        for j in range(NY):
-            ys = lax.rem(y + NY - j, NY)
-            if step < 3 or j < 2:
-                zs = lax.rem(z + NZ - step - 1, NZ)
-                send_to(plane.at[zs, ys], plane.at[zs, ys], s_up.at[step, j], r_up.at[step, j], up).wait_recv()
-                if step < 2 or (step == 2 and j < 2):
-                    pass_up(step + 1, j, zs, ys)
-            if step < 3 or j >= 2:
-                zs = lax.rem(z + step + 1, NZ)
-                send_to(plane.at[zs, ys], plane.at[zs, ys], s_down.at[step, j], r_down.at[step, j], down).wait_recv()
-                if step < 2 or (step == 2 and j >= 2):
-                    pass_down(step + 1, j, zs, ys)
-            if step == 0 and j == 0:
-                land_z(1)
-                land_z(7)
-            if step == 0 and j == 2:
-                land_z(2)
-                land_z(6)
-            if step == 1 and j == 0:
-                land_z(3)
-                land_z(5)
-                land_z(4)
-            idle(2 if step < 1 else 1)
+    for i, j in enumerate(LINE):
+        land_up(1, j)
+        land_down(1, j)
+        idle()
+        if i == 0:
+            land_z(2)
+            land_z(6)
+        idle()
+        if i == 2:
+            land_z(3)
+            land_z(5)
+            land_z(4)
+        idle()
+    for far in (0, 2, 3):
+        for j in LINE:
+            if far < 3 or j < 2:
+                land_up(far, j)
+            if far < 3 or j >= 2:
+                land_down(far, j)
+            idle()
     idle(len(pieces) - done[0])
     for n, key in enumerate(GROUP):
         slot = slot_of(*sources[key])
@@ -407,15 +445,15 @@
             send_to(upper.at[zs, ys], upper.at[zs, ys], s_uy.at[k, j - 1], r_uy.at[k, j - 1], up).wait_recv()
 
     rows = group[...].reshape(8 * 16, D + EXT)
-    low_cols = plane[...].reshape(32 * 16, H)
-    high_cols = upper[...].reshape(32 * 16, H + EXT)
-    row_main, high_main = rows[:, :D], high_cols[:, :H]
+    low_cols = plane[...].reshape(32 * 16, LOW)
+    high_cols = upper[...].reshape(32 * 16, D - LOW + EXT)
+    row_main, high_main = rows[:, :D], high_cols[:, : D - LOW]
     logit_mult = scale_ref[0]
-    products = dot_t(row_main[:, :H], low_cols) + dot_t(row_main[:, H:], high_main)
+    products = dot_t(row_main[:, :LOW], low_cols) + dot_t(row_main[:, LOW:], high_main)
     logits = logit_mult * products + bias_ref[0]
     pick = lax.broadcasted_iota(jnp.int32, (16, EXT), 0) * (EXT // 2)
     pick = jnp.where(pick == lax.broadcasted_iota(jnp.int32, (16, EXT), 1), 1.0, 0.0).astype(BF16)
-    col_extra = dot_t(pick, high_cols[:, H:])
+    col_extra = dot_t(pick, high_cols[:, D - LOW :])
     total = jnp.sum(col_extra[1:2, :]) * (1.0 / 16.0)
     col_usable = col_extra[0:1, :]
     row_usable = rows[:, D : D + 1].astype(F32)
@@ -602,7 +640,6 @@
 def run_kernel(count, logit_scale, logit_bias, loss_scale, image, text, image_weight, text_weight):
     dma = pltpu.SemaphoreType.DMA
     vmem = pl.BlockSpec(memory_space=pltpu.VMEM)
-    smem = pl.BlockSpec(memory_space=pltpu.SMEM)
     anywhere = pl.BlockSpec(memory_space=pltpu.HBM)
     image_rows, text_rows = image.shape[0], text.shape[0]
     ring = pltpu.VMEM((4, SUBS, ZROWS + 16, SUB), jnp.int16)
@@ -614,17 +651,21 @@
             jax.ShapeDtypeStruct((12, H), F32),
             jax.ShapeDtypeStruct(tile, F32),
         ),
-        in_specs=[smem, smem, smem, smem, anywhere, anywhere, anywhere, anywhere],
+        in_specs=[anywhere, anywhere, anywhere, anywhere, anywhere, anywhere, anywhere, anywhere],
         out_specs=(vmem, vmem, vmem),
         scratch_shapes=[
+            pltpu.SMEM((1,), jnp.int32),
+            pltpu.SMEM((1,), F32),
+            pltpu.SMEM((1,), F32),
+            pltpu.SMEM((1,), F32),
             pltpu.VMEM((D, H), BF16),
             pltpu.VMEM((D, H), BF16),
             pltpu.VMEM((32, H), F32),
             pltpu.VMEM((2, 8, H + EXT), F32),
             pltpu.VMEM((2, 8, H + EXT), F32),
             pltpu.VMEM((4,) + tile, F32),
-            pltpu.VMEM((NZ, NY, 16, H), BF16),
-            pltpu.VMEM((NZ, NY, 16, H + EXT), BF16),
+            pltpu.VMEM((NZ, NY, 16, LOW), BF16),
+            pltpu.VMEM((NZ, NY, 16, D - LOW + EXT), BF16),
             pltpu.VMEM((8, 16, D + EXT), BF16),
             pltpu.VMEM((4, 2, 32, H + EXT), jnp.int16),
             pltpu.VMEM((8, 32, H + EXT), jnp.int16),
@@ -655,7 +696,7 @@
             pltpu.VMEM((8,) + tile, F32),
             pltpu.VMEM((NY,) + tile, F32),
             pltpu.VMEM((NZ,) + tile, F32),
-            dma((8,)),
+            dma((12,)),
         ]
         + [dma((2,))] * 2
         + [dma((3,))] * 2

time: 89.1 us -> 87.1 us (0.978)
  Pallas kernels: 84 us -> 82 us
    pallas_call x1, Pallas kernels: 84 us -> 82 us  [run_kernel(): pl.pallas_call(kernel, out_shape=(jax.ShapeDtypeStruct((12, H), F32), jax...]
where the time goes in v5:
time: 87.1 us; the launch traced here: 87 us
  Pallas kernels  82 us (94%)
  between operations  3.22 us (4%)
  local copies, waits for them, and re-layouts  1.75 us (2%)
    pallas_call x1, Pallas kernels, run_kernel(): pl.pallas_call(kernel, out_shape=(jax.ShapeDtypeStruct((12, H), F32), jax...  82 us

profile of v5, /device:TPU:1, one launch (start us, length us, event | category | flops | bytes accessed | tf_op | source)
XLA Modules:
  0.0 87.0 jit_solution(2350103333274870792)
XLA Ops:
  3.2 82.0 %shard_map.103 = (f32[12,768]{1,0:T(8,128)S(1)}, f32[12,768]{1,0:T(8,128)S(1)}, f32[8,128]{1,0:T(8,128)S(1)}) custom-call(s32[1]{0:T(128)S(6)} %copy.16.count_hbm, f32[1]{0:T(128)S(6)} %copy.13.scale_hbm, f32[1]{0:T(128)S(6)} %copy.14.bias_hbm, f32[1]{0:T(128)S(6)} %copy.15.loss_scale_hbm, bf16[1024,1536]{1,0:T(8,128)(2,1)} %bitcast.3, ...), custom_call_target="tpu_custom_call" | custom-call | tf_op jit(solution)/shard_map/pallas_call | solution.py:647
  85.3 0.5 slice.3
  85.8 0.6 copy.17
  86.4 0.6 copy.18

commit v6 on v5

--- a/solution.py
+++ b/solution.py
@@ -99,7 +99,7 @@
 
 YX = [(dxh, j) for dxh in range(2) for j in range(NY) if (dxh, j) != (0, 0)]
 PAIRS = [(0, 1), (2, 0), (2, 1)]
-LOW = 640
+LOW = 512
 LINE = [0, 1, 3, 2]
 ORDER = [4, 3, 5, 2, 6, 1, 7, 0]
 SUBS = 4
@@ -110,10 +110,7 @@
 
 
 def kernel(
-    count_hbm,
-    scale_hbm,
-    bias_hbm,
-    loss_scale_hbm,
+    scalars_ref,
     image_ref,
     text_ref,
     image_weight_ref,
@@ -121,10 +118,6 @@
     image_out_ref,
     text_out_ref,
     loss_out_ref,
-    count_ref,
-    scale_ref,
-    bias_ref,
-    loss_scale_ref,
     image_weight,
     text_weight,
     pooled,
@@ -217,6 +210,10 @@
     twin = members[(0, 1)]
     copies = []
 
+    def flush(sent):
+        for copy in sent:
+            copy.wait_send()
+
     def start(*args):
         copy = send_to(*args)
         copy.start()
@@ -228,10 +225,6 @@
         loads[name] = pltpu.make_async_copy(src, dst, s_load.at[len(loads)])
         loads[name].start()
 
-    fetch("count", count_hbm, count_ref)
-    fetch("scale", scale_hbm, scale_ref)
-    fetch("bias", bias_hbm, bias_ref)
-    fetch("loss", loss_scale_hbm, loss_scale_ref)
     fetch("tw", text_weight_ref, text_weight)
     for p in range(2):
         at = pl.ds(256 * p, 256)
@@ -282,9 +275,7 @@
     pool(text_tok, text_pre, 1, 32, 8)
     pl.semaphore_wait(barrier, len(peers))
     swap(1)
-    for name in ("count", "scale", "bias", "loss"):
-        loads[name].wait()
-    own_count = jnp.full((8, 128), count_ref[0], jnp.int32).astype(F32)
+    own_count = jnp.broadcast_to(scalars_ref[0:1, :], (8, 128))
     counts[pair_slot] = own_count
     for n, key in enumerate(PAIRS):
         start(counts.at[pair_slot], counts.at[pair_slot], s_count.at[n], r_count.at[n], members[key])
@@ -448,9 +439,9 @@
     low_cols = plane[...].reshape(32 * 16, LOW)
     high_cols = upper[...].reshape(32 * 16, D - LOW + EXT)
     row_main, high_main = rows[:, :D], high_cols[:, : D - LOW]
-    logit_mult = scale_ref[0]
+    logit_mult = scalars_ref[1:2, 0:1]
     products = dot_t(row_main[:, :LOW], low_cols) + dot_t(row_main[:, LOW:], high_main)
-    logits = logit_mult * products + bias_ref[0]
+    logits = logit_mult * products + scalars_ref[2:3, 0:1]
     pick = lax.broadcasted_iota(jnp.int32, (16, EXT), 0) * (EXT // 2)
     pick = jnp.where(pick == lax.broadcasted_iota(jnp.int32, (16, EXT), 1), 1.0, 0.0).astype(BF16)
     col_extra = dot_t(pick, high_cols[:, D - LOW :])
@@ -466,7 +457,7 @@
     used = (row_usable * col_usable > 0.5) & (r_text != q_text)
     sign = jnp.where(same, 1.0, -1.0)
     margin = -sign * logits
-    coeff = loss_scale_ref[0] / total
+    coeff = scalars_ref[3:4, 0:1] / total
     dlogit = (jnp.where(used, -sign * jax.nn.sigmoid(margin), 0.0) * coeff).astype(BF16)
     grad = logit_mult * jnp.concatenate(
         [jnp.dot(dlogit, cols, preferred_element_type=F32) for cols in (low_cols, high_main)], axis=1
@@ -535,11 +526,11 @@
         out[step, h] = encode(value, 16)
         start(out.at[step, h], inn.at[step, h], send_sem.at[step, h], recv_sem.at[step, h], way)
 
-    def ring_step(step, n_up, n_down):
+    def ring_step(step, n_up, n_down, begin=0, end=SUBS):
         ups, downs = list(range(UPS)), list(range(UPS, SUBS))
         if step > 0:
             ups, downs = downs + ups, ups + downs
-        for i in range(SUBS):
+        for i in range(begin, end):
             if i < len(ups):
                 ring(step, n_up, ups[i], up_out, up_in, s_rup, r_rup, up, ups[i] < UPS)
             if i < len(downs):
@@ -569,18 +560,23 @@
                 line_out[k - 1] = encode(part, 8)
                 start(line_out.at[k - 1], line_in.at[k - 1], s_line.at[k - 1], r_line.at[k - 1], z_peers[k - 1])
 
+    old = copies[:]
+    del copies[:]
     compute(0)
     compute(1)
     chunk(0)
     ring_step(0, 0, 0)
     compute(2)
     compute(3)
-    for n in (1, 2, 3):
+    for n in (1, 2):
         chunk(n)
+    ring_step(1, 1, 2, 0, UPS)
+    flush(old)
+    chunk(3)
     spread(0)
     compute(4)
     compute(5)
-    ring_step(1, 1, 2)
+    ring_step(1, 1, 2, UPS)
     compute(6)
     compute(7)
     for n in (4, 5, 6, 7):
@@ -600,10 +596,9 @@
         start(loss_z.at[0], loss_z.at[k], s_lz.at[k - 1], r_lz.at[k - 1], z_peers[k - 1])
     ring_step(3, 5, 6)
     collect(1)
-    for copy in copies:
-        copy.wait_send()
+    old = copies[:]
     del copies[:]
-    for h in range(SUBS):
+    for h in (0, 2, 1, 3):
         at = slice(h * SUB, h * SUB + SUB)
         value = terms[7, :, at]
         send_to(up_out.at[3, h], up_in.at[3, h], s_rup.at[3, h], r_rup.at[3, h], up).wait_recv()
@@ -615,29 +610,29 @@
     for n, (dxh, j) in enumerate(YX):
         src = near_out.at[lax.rem(xh + dxh, 2) * NY + lax.rem(y + j, NY)]
         start(src, near_in.at[n], s_near.at[n], r_near.at[n], near[(dxh, j)])
+    flush(old)
     rest = rest_own[...]
     for k in range(1, NZ):
         send_to(line_in.at[k - 1], line_in.at[k - 1], s_line.at[k - 1], r_line.at[k - 1], z_peers[k - 1]).wait_recv()
         rest = rest + decode(line_in[k - 1], 8)
     final[c, :, FAR:] = rest
+    for k in range(1, NZ):
+        send_to(loss_z.at[0], loss_z.at[k], s_lz.at[k - 1], r_lz.at[k - 1], z_peers[k - 1]).wait_recv()
+    loss_out_ref[...] = jnp.sum(loss_z[...], axis=0)
     result = decode(near_out[xh * NY + y], 8)
     for n, key in enumerate(YX):
         send_to(near_in.at[n], near_in.at[n], s_near.at[n], r_near.at[n], near[key]).wait_recv()
         result = result + decode(near_in[n], 8)
-    for k in range(1, NZ):
-        send_to(loss_z.at[0], loss_z.at[k], s_lz.at[k - 1], r_lz.at[k - 1], z_peers[k - 1]).wait_recv()
-    loss_out_ref[...] = jnp.sum(loss_z[...], axis=0)
     final[c, :, :FAR] = result
     start(final.at[c], final.at[c], s_final, r_final, twin)
     send_to(final.at[1 - c], final.at[1 - c], s_final, r_final, twin).wait_recv()
     even = c == 0
     image_out_ref[...] = jnp.where(even, final[0, 0:12, :], final[0, 12:24, :])
     text_out_ref[...] = jnp.where(even, final[1, 0:12, :], final[1, 12:24, :])
-    for copy in copies:
-        copy.wait_send()
-
-
-def run_kernel(count, logit_scale, logit_bias, loss_scale, image, text, image_weight, text_weight):
+    flush(copies)
+
+
+def run_kernel(scalars, image, text, image_weight, text_weight):
     dma = pltpu.SemaphoreType.DMA
     vmem = pl.BlockSpec(memory_space=pltpu.VMEM)
     anywhere = pl.BlockSpec(memory_space=pltpu.HBM)
@@ -651,13 +646,9 @@
             jax.ShapeDtypeStruct((12, H), F32),
             jax.ShapeDtypeStruct(tile, F32),
         ),
-        in_specs=[anywhere, anywhere, anywhere, anywhere, anywhere, anywhere, anywhere, anywhere],
+        in_specs=[vmem, anywhere, anywhere, anywhere, anywhere],
         out_specs=(vmem, vmem, vmem),
         scratch_shapes=[
-            pltpu.SMEM((1,), jnp.int32),
-            pltpu.SMEM((1,), F32),
-            pltpu.SMEM((1,), F32),
-            pltpu.SMEM((1,), F32),
             pltpu.VMEM((D, H), BF16),
             pltpu.VMEM((D, H), BF16),
             pltpu.VMEM((32, H), F32),
@@ -696,7 +687,7 @@
             pltpu.VMEM((8,) + tile, F32),
             pltpu.VMEM((NY,) + tile, F32),
             pltpu.VMEM((NZ,) + tile, F32),
-            dma((12,)),
+            dma((8,)),
         ]
         + [dma((2,))] * 2
         + [dma((3,))] * 2
@@ -718,7 +709,7 @@
         compiler_params=pltpu.CompilerParams(
             collective_id=1, has_side_effects=True, vmem_limit_bytes=53 * 1024 * 1024
         ),
-    )(count, logit_scale, logit_bias, loss_scale, image, text, image_weight, text_weight)
+    )(scalars, image, text, image_weight, text_weight)
 
 
 def body(
@@ -731,11 +722,11 @@
     loss_scale,
     valid_count,
 ):
+    row = lax.broadcasted_iota(jnp.int32, (8, 128), 0)
+    scalars = jnp.where(row == 0, valid_count[0].astype(F32), logit_scale[0])
+    scalars = jnp.where(row == 2, logit_bias[0], jnp.where(row == 3, loss_scale[0], scalars))
     image_grad, text_grad, loss = run_kernel(
-        valid_count,
-        logit_scale,
-        logit_bias,
-        loss_scale,
+        scalars,
         image_tokens.reshape(-1, D),
         text_tokens.reshape(-1, D),
         image_weight,

time: 87.1 us -> 86.4 us (level)
  no operation moved by 1% of the time
where the time goes in v6:
time: 86.4 us; the launch traced here: 86.3 us
  Pallas kernels  81.2 us (94%)
  between operations  3.24 us (4%)
  local copies, waits for them, and re-layouts  1.75 us (2%)
    pallas_call x1, Pallas kernels, run_kernel(): pl.pallas_call(kernel, out_shape=(jax.ShapeDtypeStruct((12, H), F32), jax...  81.2 us

profile of v6, /device:TPU:1, one launch (start us, length us, event | category | flops | bytes accessed | tf_op | source)
XLA Modules:
  0.0 86.3 jit_solution(16031523874175155711)
XLA Ops:
  3.2 0.1 select_select_fusion.scalars_ref
  3.3 81.2 %shard_map.103 = (f32[12,768]{1,0:T(8,128)S(1)}, f32[12,768]{1,0:T(8,128)S(1)}, f32[8,128]{1,0:T(8,128)S(1)}) custom-call(f32[8,128]{1,0:T(8,128)S(1)} %select_select_fusion.scalars_ref, bf16[1024,1536]{1,0:T(8,128)(2,1)} %bitcast.10, bf16[512,1536]{1,0:T(8,128)(2,1)} %bitcast.11, bf16[1536,768]{1,0:T(8,128)(2,1)} %image_weight_ref.1, ...), custom_call_target="tpu_custom_call" | custom-call | tf_op jit(solution)/shard_map/pallas_call | solution.py:642
  84.5 0.5 slice.3
  85.0 0.6 copy.17
  85.6 0.6 copy.18
  (2 shorter events, 0.0 us)

commit v7 on v6

--- a/solution.py
+++ b/solution.py
@@ -225,10 +225,11 @@
         loads[name] = pltpu.make_async_copy(src, dst, s_load.at[len(loads)])
         loads[name].start()
 
-    fetch("tw", text_weight_ref, text_weight)
-    for p in range(2):
-        at = pl.ds(256 * p, 256)
-        fetch("t%d" % p, text_ref.at[at], text_tok.at[at])
+    left, right = pl.ds(0, H // 2), pl.ds(H // 2, H // 2)
+    fetch("t0", text_ref.at[pl.ds(0, 256)], text_tok.at[pl.ds(0, 256)])
+    fetch("tw", text_weight_ref.at[:, left], text_weight.at[:, left])
+    fetch("tx", text_weight_ref.at[:, right], text_weight.at[:, right])
+    fetch("t1", text_ref.at[pl.ds(256, 256)], text_tok.at[pl.ds(256, 256)])
     fetch("iw", image_weight_ref, image_weight)
     for p in range(4):
         at = pl.ds(256 * p, 256)
@@ -240,9 +241,9 @@
 
     columns = pl.ds(pl.multiple_of(lo * H, H), H)
 
-    def forward(tok, weight, pre, p):
-        at = slice(256 * p, 256 * p + 256)
-        pre[at, :] = jnp.dot(tok[at, :], weight[...], preferred_element_type=F32)
+    def forward(tok, weight, pre, p, begin=0, end=H):
+        at, cols = slice(256 * p, 256 * p + 256), slice(begin, end)
+        pre[at, cols] = jnp.dot(tok[at, :], weight[:, cols], preferred_element_type=F32)
 
     def pool(tok, pre, p, tokens, offset):
         for i in range(256 // tokens):
@@ -263,9 +264,11 @@
         half_out[w, :, H:] = jnp.broadcast_to(squares, (8, EXT))
         start(half_out.at[w], half_in.at[w], s_other.at[w], r_other.at[w], partner)
 
-    for name in ("tw", "t0"):
+    for name in ("t0", "tw"):
         loads[name].wait()
-    forward(text_tok, text_weight, text_pre, 0)
+    forward(text_tok, text_weight, text_pre, 0, 0, H // 2)
+    loads["tx"].wait()
+    forward(text_tok, text_weight, text_pre, 0, H // 2, H)
     loads["t1"].wait()
     forward(text_tok, text_weight, text_pre, 1)
     pool(text_tok, text_pre, 0, 32, 8)
@@ -687,7 +690,7 @@
             pltpu.VMEM((8,) + tile, F32),
             pltpu.VMEM((NY,) + tile, F32),
             pltpu.VMEM((NZ,) + tile, F32),
-            dma((8,)),
+            dma((9,)),
         ]
         + [dma((2,))] * 2
         + [dma((3,))] * 2

time: 86.4 us -> 86.3 us (level)
  no operation moved by 1% of the time
where the time goes in v7:
time: 86.3 us; the launch traced here: 86.2 us
  Pallas kernels  81.1 us (94%)
  between operations  3.24 us (4%)
  local copies, waits for them, and re-layouts  1.75 us (2%)
    pallas_call x1, Pallas kernels, run_kernel(): pl.pallas_call(kernel, out_shape=(jax.ShapeDtypeStruct((12, H), F32), jax...  81.1 us

profile of v7, /device:TPU:1, one launch (start us, length us, event | category | flops | bytes accessed | tf_op | source)
XLA Modules:
  0.0 86.2 jit_solution(15666385976304193330)
XLA Ops:
  3.2 0.1 select_select_fusion.scalars_ref
  3.3 81.1 %shard_map.103 = (f32[12,768]{1,0:T(8,128)S(1)}, f32[12,768]{1,0:T(8,128)S(1)}, f32[8,128]{1,0:T(8,128)S(1)}) custom-call(f32[8,128]{1,0:T(8,128)S(1)} %select_select_fusion.scalars_ref, bf16[1024,1536]{1,0:T(8,128)(2,1)} %bitcast.10, bf16[512,1536]{1,0:T(8,128)(2,1)} %bitcast.11, bf16[1536,768]{1,0:T(8,128)(2,1)} %image_weight_ref.1, ...), custom_call_target="tpu_custom_call" | custom-call | tf_op jit(solution)/shard_map/pallas_call | solution.py:645
  84.4 0.5 slice.3
  84.9 0.6 copy.17
  85.5 0.6 copy.18
  (2 shorter events, 0.0 us)
